TPU v7x, 512 devices: a whole 4x4x16 slice. The times are simulated.
512 devices in a mesh: head: 8 (over x, core), ctx: 64 (over z, y).
Axes of the slice: x: 4, y: 4, z: 16, core: 2. Of those that a mesh axis runs over, the one named last changes fastest.
Arguments:
- queries: bfloat16 [32768, 8192], P(('ctx', 'head')), may hold values from -6 to 6
- outputs: bfloat16 [32768, 8192], P(('ctx', 'head')), may hold values from -6 to 6
- output_gradient: bfloat16 [32768, 8192], P(('ctx', 'head')), may hold values from -6 to 6
- keys: bfloat16 [32768, 1024], P(('ctx', 'head')), may hold values from -6 to 6
- values: bfloat16 [32768, 1024], P(('ctx', 'head')), may hold values from -6 to 6
- log_row_norm: float32 [32768, 64], P(('ctx', 'head')), may hold values from 4 to 7
- kv_index: int32 [256, 10], replicated, may hold values from 0 to 255, as said below
- counts: int32 [256], replicated, may hold values from 1 to 10
Outputs:
- grad_queries: bfloat16 [32768, 8192], P(('ctx', 'head'))
- key_gradient: bfloat16 [32768, 1024], P(('ctx', 'head'))
- value_gradient: bfloat16 [32768, 1024], P(('ctx', 'head'))
Inputs may be any that keep to these rules, and one draw needn't show every extreme that they name: `kv_index`: row i lists distinct tiles of index at most i in rising order in its first counts[i] entries: always i, i - 1 when i >= 1, and tile 3 when i >= 3, besides others; the remaining entries are 0. Tile t lies on ctx index t // 4. Taken together, the rows of the tiles of one ctx index name at most one tile of each other ctx index.
All inputs are finite; a program needn't handle non-finite values.
Results may differ from a plain program's by a relative error of at most 0.0049.
Values may be sent and summed in bfloat16 or wider, within the bound.
A program may use at most 128 MiB of HBM per device.

v0:
```python
import jax
import jax.numpy as jnp
from jax import lax
from jax.sharding import PartitionSpec as P

QUERY_HEADS = 64
KEY_VALUE_HEADS = 8
HEAD_SIZE = 128
TILE_TOKENS = 128


def pairwise_terms(
    query_row_block,
    gradient_rows,
    row_norm_block,
    delta_row_block,
    pair_tile,
    on_diagonal,
    kv_heads,
):
    scale_factor = HEAD_SIZE ** (-0.5)
    key_value = pair_tile.reshape(TILE_TOKENS, kv_heads, 2 * HEAD_SIZE)
    key_part = key_value[:, :, :HEAD_SIZE]
    value_part = key_value[:, :, HEAD_SIZE:]
    scores = (
        jnp.einsum("qagd,kad->agqk", query_row_block, key_part, preferred_element_type=jnp.float32)
        * scale_factor
    )
    positions = jnp.arange(TILE_TOKENS, dtype=jnp.int32)
    allowed = (positions[None, :] <= positions[:, None]) | jnp.logical_not(on_diagonal)
    norm_shift = jnp.transpose(row_norm_block, (1, 2, 0))[:, :, :, None]
    weights = jnp.where(allowed, jnp.exp(scores - norm_shift), jnp.float32(0.0))
    rounded = weights.astype(jnp.bfloat16)
    value_grad = jnp.einsum(
        "agqk,qagd->kad", rounded, gradient_rows, preferred_element_type=jnp.float32
    )
    prob_grad = jnp.einsum(
        "qagd,kad->agqk", gradient_rows, value_part, preferred_element_type=jnp.float32
    )
    delta_shift = jnp.transpose(delta_row_block, (1, 2, 0))[:, :, :, None]
    score_grad = (weights * (prob_grad - delta_shift)).astype(jnp.bfloat16)
    query_gradient = scale_factor * jnp.einsum(
        "agqk,kad->qagd", score_grad, key_part, preferred_element_type=jnp.float32
    )
    key_grad = scale_factor * jnp.einsum(
        "agqk,qagd->kad", score_grad, query_row_block, preferred_element_type=jnp.float32
    )
    pairwise_gradient = jnp.concatenate([key_grad, value_grad], axis=2).reshape(
        TILE_TOKENS, kv_heads * 2 * HEAD_SIZE
    )
    return (query_gradient, pairwise_gradient)


def on_device(queries, outputs, output_gradient, keys, values, log_row_norm, kv_index, counts):
    token_rows = queries.shape[0]
    delta_value = jnp.sum(
        (output_gradient.astype(jnp.float32) * outputs.astype(jnp.float32)).reshape(
            token_rows, QUERY_HEADS, HEAD_SIZE
        ),
        axis=2,
    )
    query_all, grad_all, key_all, value_all = (
        lax.all_to_all(queries, "head", split_axis=1, concat_axis=0, tiled=True),
        lax.all_to_all(output_gradient, "head", split_axis=1, concat_axis=0, tiled=True),
        lax.all_to_all(keys, "head", split_axis=1, concat_axis=0, tiled=True),
        lax.all_to_all(values, "head", split_axis=1, concat_axis=0, tiled=True),
    )
    norm_all, delta_all = (
        lax.all_to_all(log_row_norm, "head", split_axis=1, concat_axis=0, tiled=True),
        lax.all_to_all(delta_value, "head", split_axis=1, concat_axis=0, tiled=True),
    )
    ctx_count = lax.axis_size("ctx")
    device = lax.axis_index("ctx")
    seq_rows = query_all.shape[0]
    tiles = seq_rows // TILE_TOKENS
    kv_local = key_all.shape[1] // HEAD_SIZE
    query_group = QUERY_HEADS // KEY_VALUE_HEADS
    query_tile_block = query_all.reshape(tiles, TILE_TOKENS, kv_local, query_group, HEAD_SIZE)
    gradient_tiles = grad_all.reshape(tiles, TILE_TOKENS, kv_local, query_group, HEAD_SIZE)
    tile_norm_block = norm_all.reshape(tiles, TILE_TOKENS, kv_local, query_group)
    delta_tile_block = delta_all.reshape(tiles, TILE_TOKENS, kv_local, query_group)
    own_pairs = jnp.concatenate(
        [
            key_all.reshape(tiles, TILE_TOKENS, kv_local, HEAD_SIZE),
            value_all.reshape(tiles, TILE_TOKENS, kv_local, HEAD_SIZE),
        ],
        axis=3,
    ).reshape(tiles, TILE_TOKENS, kv_local * 2 * HEAD_SIZE)
    width = own_pairs.shape[2]
    owned = device * tiles + jnp.arange(tiles, dtype=jnp.int32)
    listed = jnp.arange(kv_index.shape[1], dtype=jnp.int32)[None, :] < counts[:, None]
    hits = jnp.any((kv_index[:, :, None] == owned[None, None, :]) & listed[:, :, None], axis=1)
    wanted = (
        jnp.any(hits.reshape(ctx_count, tiles, tiles), axis=1)
        & (jnp.arange(ctx_count, dtype=jnp.int32) != device)[:, None]
    )
    selector = wanted.astype(jnp.bfloat16)
    outgoing = (
        jnp.dot(
            selector,
            own_pairs.reshape(tiles, TILE_TOKENS * width),
            preferred_element_type=jnp.float32,
        )
        .astype(jnp.bfloat16)
        .reshape(ctx_count, TILE_TOKENS, width)
    )
    incoming = lax.all_to_all(outgoing, "ctx", split_axis=0, concat_axis=0, tiled=True)
    candidates = jnp.concatenate([own_pairs, incoming], axis=0)

    def locate(target_device):
        holder = target_device // tiles
        return jnp.where(holder == device, target_device - device * tiles, tiles + holder)

    initial_carry = (
        jnp.zeros((tiles, TILE_TOKENS, kv_local, query_group, HEAD_SIZE), jnp.float32),
        jnp.zeros((candidates.shape[0], TILE_TOKENS, width), jnp.float32),
    )
    status = initial_carry
    for index in range(tiles):
        query_tile = device * tiles + index

        def entry(position, state, index=index, query_tile=query_tile):
            target_device = kv_index[query_tile, position]
            place = locate(target_device)
            query_sums, pair_sums = state
            pair_tile = lax.dynamic_index_in_dim(candidates, place, 0, keepdims=False)
            query_gradient, pairwise_gradient = pairwise_terms(
                query_tile_block[index],
                gradient_tiles[index],
                tile_norm_block[index],
                delta_tile_block[index],
                pair_tile,
                target_device == query_tile,
                kv_local,
            )
            return (
                query_sums.at[index].add(query_gradient),
                pair_sums.at[place].add(pairwise_gradient),
            )

        status = lax.fori_loop(0, counts[query_tile], entry, status)
    returned = lax.all_to_all(
        status[1][tiles : tiles + ctx_count], "ctx", split_axis=0, concat_axis=0, tiled=True
    )
    query_sums, pair_sums = status
    gathered_terms = jnp.dot(
        jnp.transpose(selector.astype(jnp.float32)),
        returned.reshape(ctx_count, TILE_TOKENS * width),
        precision=lax.Precision.HIGHEST,
        preferred_element_type=jnp.float32,
    )
    owner_sums = pair_sums[:tiles] + gathered_terms.reshape(tiles, TILE_TOKENS, width)
    pairwise_output = owner_sums.astype(jnp.bfloat16).reshape(seq_rows, kv_local, 2 * HEAD_SIZE)
    key_grads = pairwise_output[:, :, :HEAD_SIZE].reshape(seq_rows, kv_local * HEAD_SIZE)
    value_grads = pairwise_output[:, :, HEAD_SIZE:].reshape(seq_rows, kv_local * HEAD_SIZE)
    query_grads = query_sums.astype(jnp.bfloat16).reshape(
        seq_rows, kv_local * query_group * HEAD_SIZE
    )
    grad_queries, key_gradient, value_gradient = (
        lax.all_to_all(query_grads, "head", split_axis=0, concat_axis=1, tiled=True),
        lax.all_to_all(key_grads, "head", split_axis=0, concat_axis=1, tiled=True),
        lax.all_to_all(value_grads, "head", split_axis=0, concat_axis=1, tiled=True),
    )
    return (grad_queries, key_gradient, value_gradient)


def solution(mesh):
    placed = (
        P(("ctx", "head"), None),
        P(("ctx", "head"), None),
        P(("ctx", "head"), None),
        P(("ctx", "head"), None),
        P(("ctx", "head"), None),
        P(("ctx", "head"), None),
        P(),
        P(),
    )
    return jax.shard_map(
        on_device,
        mesh=mesh,
        in_specs=placed,
        out_specs=(P(("ctx", "head"), None), P(("ctx", "head"), None), P(("ctx", "head"), None)),
        check_vma=False,
    )
```

profile of v0, /device:TPU:1, one launch (start us, length us, event | category | flops | bytes accessed | tf_op | source)
XLA Modules:
  0.0 1272.0 jit_solution(16137007650512731459)
XLA Ops:
  2.2 10.1 all-to-all-start.4
  17.0 3.9 all-to-all-start.6
  21.6 4.0 all-to-all-done.6
  25.6 4.0 all-to-all-start
  30.3 4.6 all-to-all-done
  34.9 4.1 all-to-all-start.1
  39.1 2.3 copy.378
  41.3 3.0 all-to-all-done.1
  44.4 4.3 all-to-all-start.3
  49.8 14.0 %all-to-all-done.3 = bf16[64,8,1024]{2,0,1:T(8,128)(2,1)S(1)} async-done(((bf16[64,8,1024]{2,0,1:T(8,128)(2,1)}), bf16[64,8,1024]{2,0,1:T(8,128)(2,1)S(1)}, u32[]{:S(2)}, u32[]{:S(2)}) %all-to-all-start.3) | async-done | bytes 1048608 | tf_op jit(solution)/shard_map/all_to_all | solution.py:63
  63.8 4.3 all-to-all-start.5
  71.1 3.0 copy.357
  74.1 9.1 all-to-all-done.5
  83.3 14.4 %all-to-all-start.2 = ((bf16[64,128,256]{2,1,0:T(8,128)(2,1)}), bf16[64,128,256]{2,1,0:T(8,128)(2,1)}, u32[]{:S(2)}, u32[]{:S(2)}) async-start(bf16[64,128,256]{2,1,0:T(8,128)(2,1)} %bitcast.692), calls=%async_computation.2 | async-start | bytes 8388608 | tf_op jit(solution)/shard_map/all_to_all | solution.py:107
  103.2 178.1 %all-to-all-done.2 = bf16[64,128,256]{2,1,0:T(8,128)(2,1)} async-done(((bf16[64,128,256]{2,1,0:T(8,128)(2,1)}), bf16[64,128,256]{2,1,0:T(8,128)(2,1)}, u32[]{:S(2)}, u32[]{:S(2)}) %all-to-all-start.2) | async-done | bytes 4194336 | tf_op jit(solution)/shard_map/all_to_all | solution.py:107
  281.3 4.6 pad_maximum_fusion
  286.2 4.6 broadcast_in_dim.85
  290.8 14.6 %while.65 = (s32[]{:T(128)}, f32[4,128,1,8,128]{1,4,3,2,0:T(8,128)S(1)}, f32[68,128,256]{1,2,0:T(8,128)}, s32[]{:T(128)}, s32[256,10]{0,1:T(8,128)}, /*index=5*/...) while((s32[]{:T(128)}, ...), condition=%wide.region_5.6_spmd, body=%wide.region_3.5_spmd.sunk | while | flops 169099312 | bytes 5269006 | solution.py:141
  305.3 27.8 %while.66 = (s32[]{:T(128)}, f32[4,128,1,8,128]{1,4,3,2,0:T(8,128)S(1)}, f32[68,128,256]{1,2,0:T(8,128)}, s32[]{:T(128)}, s32[256,10]{0,1:T(8,128)}, /*index=5*/...) while((s32[]{:T(128)}, ...), condition=%wide.region_8.9_spmd, body=%wide.region_6.8_spmd.sunk | while | flops 169099312 | bytes 5269014 | solution.py:141
  333.1 27.1 %while.67 = (s32[]{:T(128)}, f32[4,128,1,8,128]{1,4,3,2,0:T(8,128)S(1)}, f32[68,128,256]{1,2,0:T(8,128)}, s32[]{:T(128)}, s32[256,10]{0,1:T(8,128)}, /*index=5*/...) while((s32[]{:T(128)}, ...), condition=%wide.region_11.12_spmd, body=%wide.region_9.11_spmd.sunk | while | flops 169099312 | bytes 5269014 | solution.py:141
  360.2 27.6 %while.68 = (s32[]{:T(128)}, f32[4,128,1,8,128]{1,4,3,2,0:T(8,128)S(1)}, f32[68,128,256]{1,2,0:T(8,128)}, s32[]{:T(128)}, s32[256,10]{0,1:T(8,128)}, /*index=5*/...) while((s32[]{:T(128)}, ...), condition=%wide.region_14.15_spmd, body=%wide.region_12.14_spmd.sunk | while | flops 169099312 | bytes 5269014 | solution.py:141
  387.8 7.6 slice.376
  395.4 456.3 %all-to-all-start.8 = ((f32[64,128,256]{1,2,0:T(8,128)}), f32[64,128,256]{1,2,0:T(8,128)}, u32[]{:S(2)}, u32[]{:S(2)}) async-start(f32[64,128,256]{1,2,0:T(8,128)} %slice.376), calls=%async_computation.8 | async-start | bytes 16777216 | tf_op jit(solution)/shard_map/all_to_all | solution.py:142
  853.9 357.0 %all-to-all-done.8 = f32[64,128,256]{1,2,0:T(8,128)} async-done(((f32[64,128,256]{1,2,0:T(8,128)}), f32[64,128,256]{1,2,0:T(8,128)}, u32[]{:S(2)}, u32[]{:S(2)}) %all-to-all-start.8) | async-done | bytes 8388640 | tf_op jit(solution)/shard_map/all_to_all | solution.py:142
  1210.9 15.1 %all-to-all-start.7 = ((bf16[8,64,1024]{2,1,0:T(8,128)(2,1)}), bf16[8,64,1024]{2,1,0:T(8,128)(2,1)S(1)}, u32[]{:S(2)}, u32[]{:S(2)}) async-start(bf16[8,64,1024]{2,1,0:T(8,128)(2,1)} %all_to_all.139), calls=%async_computation.7 | async-start | bytes 2097152 | tf_op jit(solution)/shard_map/all_to_all | solution.py:160
  1225.9 9.5 copy.313
  1235.4 9.2 copy.361
  1244.6 6.4 fusion.106
  1251.8 4.8 all-to-all-start.9
  1257.7 4.2 all-to-all-done.9
  1261.9 4.1 all-to-all-start.10
  1266.7 4.6 all-to-all-done.10
  (157 shorter events, 85.8 us)
Async XLA Ops:
  0.6 20.3 %copy-start = (bf16[64,1024]{1,0:T(8,128)(2,1)S(1)}, bf16[64,1024]{1,0:T(8,128)(2,1)}, u32[]{:S(2)}) copy-start(bf16[64,1024]{1,0:T(8,128)(2,1)} %param.35) | copy-start | bytes 393220
  2.2 14.8 %all-to-all-start.4 = ((f32[8,1,512]{2,1,0:T(1,128)}), f32[8,1,512]{2,1,0:T(1,128)S(1)}, u32[]{:S(2)}, u32[]{:S(2)}) async-start(f32[8,1,512]{2,1,0:T(1,128)} %reshape.877), calls=%async_computation.4 | async-start | bytes 32768 | tf_op jit(solution)/shard_map/all_to_all | solution.py:69
  14.1 15.5 %copy-start.5 = (bf16[64,1024]{1,0:T(8,128)(2,1)S(1)}, bf16[64,1024]{1,0:T(8,128)(2,1)}, u32[]{:S(2)}) copy-start(bf16[64,1024]{1,0:T(8,128)(2,1)} %param.36) | copy-start | bytes 393220
  14.5 34.2 %copy-start.2 = (bf16[64,8192]{1,0:T(8,128)(2,1)S(1)}, bf16[64,8192]{1,0:T(8,128)(2,1)}, u32[]{:S(2)}) copy-start(bf16[64,8192]{1,0:T(8,128)(2,1)} %param.34) | copy-start | bytes 3145732
  17.0 8.6 all-to-all-start.6
  25.6 9.3 copy-start.6
  25.6 9.3 all-to-all-start
  29.6 38.5 %copy-start.9 = (s32[256]{0:T(256)S(1)}, s32[256]{0:T(256)}, u32[]{:S(2)}) copy-start(s32[256]{0:T(256)} %param.39) | copy-start | bytes 3076
  29.6 38.5 %copy-start.8 = (s32[256,10]{0,1:T(8,128)S(1)}, s32[256,10]{0,1:T(8,128)}, u32[]{:S(2)}) copy-start(s32[256,10]{0,1:T(8,128)} %param.38) | copy-start | bytes 30724
  34.9 9.4 all-to-all-start.1
  44.4 24.3 %copy-start.3 = (bf16[64,8,128]{2,0,1:T(8,128)(2,1)}, bf16[64,8,128]{2,0,1:T(8,128)(2,1)S(1)}, u32[]{:S(2)}) copy-start(bf16[64,8,128]{2,0,1:T(8,128)(2,1)S(1)} %all-to-all-done.1) | copy-start | bytes 393220
  44.4 19.4 %all-to-all-start.3 = ((bf16[64,8,1024]{2,0,1:T(8,128)(2,1)}), bf16[64,8,1024]{2,0,1:T(8,128)(2,1)S(1)}, u32[]{:S(2)}, u32[]{:S(2)}) async-start(bf16[64,8,1024]{2,0,1:T(8,128)(2,1)} %bitcast.515), calls=%async_computation.3 | async-start | bytes 2097152 | tf_op jit(solution)/shard_map/all_to_all | solution.py:63
  63.8 19.4 %all-to-all-start.5 = ((bf16[64,8,1024]{2,0,1:T(8,128)(2,1)}), bf16[64,8,1024]{2,0,1:T(8,128)(2,1)S(1)}, u32[]{:S(2)}, u32[]{:S(2)}) async-start(bf16[64,8,1024]{2,0,1:T(8,128)(2,1)} %bitcast.514), calls=%async_computation.5 | async-start | bytes 2097152 | tf_op jit(solution)/shard_map/all_to_all | solution.py:64
  68.6 5.5 copy-start.11
  68.6 5.5 copy-start.13
  74.1 23.5 %copy-start.10 = (s32[256]{0:T(256)S(1)}, s32[256]{0:T(256)}, u32[]{:S(2)}) copy-start(s32[256]{0:T(256)} %param.39) | copy-start | bytes 3076
  74.1 25.6 %copy-start.7 = (f32[8,1,512]{2,1,0:T(1,128)S(1)}, f32[8,1,512]{2,1,0:T(1,128)}, u32[]{:S(2)}) copy-start(f32[8,1,512]{2,1,0:T(1,128)} %copy-done.6) | copy-start | bytes 49156
  83.3 198.0 %all-to-all-start.2 = ((bf16[64,128,256]{2,1,0:T(8,128)(2,1)}), bf16[64,128,256]{2,1,0:T(8,128)(2,1)}, u32[]{:S(2)}, u32[]{:S(2)}) async-start(bf16[64,128,256]{2,1,0:T(8,128)(2,1)} %bitcast.692), calls=%async_computation.2 | async-start | bytes 8388608 | tf_op jit(solution)/shard_map/all_to_all | solution.py:107
  286.2 4.6 copy-start.4
  395.4 815.4 %all-to-all-start.8 = ((f32[64,128,256]{1,2,0:T(8,128)}), f32[64,128,256]{1,2,0:T(8,128)}, u32[]{:S(2)}, u32[]{:S(2)}) async-start(f32[64,128,256]{1,2,0:T(8,128)} %slice.376), calls=%async_computation.8 | async-start | bytes 16777216 | tf_op jit(solution)/shard_map/all_to_all | solution.py:142
  1210.9 41.0 %all-to-all-start.7 = ((bf16[8,64,1024]{2,1,0:T(8,128)(2,1)}), bf16[8,64,1024]{2,1,0:T(8,128)(2,1)S(1)}, u32[]{:S(2)}, u32[]{:S(2)}) async-start(bf16[8,64,1024]{2,1,0:T(8,128)(2,1)} %all_to_all.139), calls=%async_computation.7 | async-start | bytes 2097152 | tf_op jit(solution)/shard_map/all_to_all | solution.py:160
  1235.4 9.2 copy-start.12
  1235.4 9.2 copy-start.14
  1244.6 27.4 %copy-start.1 = (bf16[64,1024]{1,0:T(8,128)(2,1)S(1)}, bf16[64,1024]{1,0:T(8,128)(2,1)}, u32[]{:S(2)}) copy-start(bf16[64,1024]{1,0:T(8,128)(2,1)} %param.35) | copy-start | bytes 393220
  1251.8 10.1 all-to-all-start.9
  1261.9 9.4 all-to-all-start.10
where the time goes:
time: 1280 us; the launch traced here: 1270 us
  waiting for transfers between devices  580 us (45%)
  starting transfers between devices  526 us (41%)
  local copies, waits for them, and re-layouts  71.2 us (6%)
  loops' own time  33.8 us (3%)
  other arithmetic  30.4 us (2%)
  matrix products  30.3 us (2%)
    all_to_all x1, starting transfers between devices, on_device(): lax.all_to_all(status[1][tiles:tiles + ctx_count], 'ctx', split_axis=0, c...  456 us
    all_to_all x1, waiting for transfers between devices, on_device(): lax.all_to_all(status[1][tiles:tiles + ctx_count], 'ctx', split_axis=0, c...  357 us
    all_to_all x1, waiting for transfers between devices, on_device(): lax.all_to_all(outgoing, 'ctx', split_axis=0, concat_axis=0, tiled=True)  178 us
    another operation x4, loops' own time, on_device(): status = lax.fori_loop(0, counts[query_tile], entry, status)  33.8 us
  transfers between devices with their start and end apart: 11, of which 10 were waited for; matrix products, arithmetic and copies ran while one was open for 4% of the time, Pallas kernels for 0%

commit v1 on v0

v1 whole, which is shorter than its diff:
```python
import functools
import math

import jax
import jax.numpy as jnp
from jax import lax
from jax.experimental import pallas as pl
from jax.experimental.pallas import tpu as pltpu
from jax.sharding import PartitionSpec as P

QUERY_HEADS = 64
KEY_VALUE_HEADS = 8
HEAD_SIZE = 128
TILE = 128
GROUP = QUERY_HEADS // KEY_VALUE_HEADS
TILES = 4
NZ = 16
NY = 4
NH = 8
ROWS = 64
WIDE = GROUP * HEAD_SIZE
UP = NZ // 2
DOWN = NZ - 1 - UP
SCALE = HEAD_SIZE ** (-0.5)
LOG2E = math.log2(math.e)
MESH = pl.DeviceIdType.MESH
F32 = jnp.float32
BF16 = jnp.bfloat16


def position():
    ctx = lax.axis_index("ctx")
    return lax.axis_index("head"), ctx // NY, lax.rem(ctx, NY)


def entry_barrier(h, z, y):
    barrier = pltpu.get_barrier_semaphore()

    def signal(**where):
        pl.semaphore_signal(barrier, inc=1, device_id=where, device_id_type=MESH)

    for d in range(1, NH):
        signal(head=lax.rem(h + d, NH))
    for d in range(1, NY):
        signal(ctx=z * NY + lax.rem(y + d, NY))
    signal(ctx=lax.rem(z + 1, NZ) * NY + y)
    signal(ctx=lax.rem(z + NZ - 1, NZ) * NY + y)
    pl.semaphore_wait(barrier, NH + NY)


def make_selection(z, y, lists_ref, sel_ref):
    slot = lax.broadcasted_iota(jnp.int32, (NZ, 128), 0)
    plane = lax.rem(z - slot + NZ, NZ)
    for dy in range(NY):
        node = z * NY + lax.rem(y + dy, NY)
        entries = lists_ref[pl.ds(node, 1), :]
        match = (entries >> 2) == plane * NY + y
        found = jnp.max(jnp.where(match, entries & 3, -1), axis=1, keepdims=True)
        sel_ref[dy] = jnp.broadcast_to(found, (NZ, 128))


def forward_kernel(
    q_ref, do_ref, k_ref, v_ref, st_ref, lists_ref,
    qh_ref, doh_ref, sth_ref, kv_ref,
    gath, picked, sel,
    x_send, x_recv, local, u_send, u_recv, d_send, d_recv, y_send, y_recv, out_sem,
):
    h, z, y = position()
    above = lax.rem(z + 1, NZ) * NY + y
    below = lax.rem(z + NZ - 1, NZ) * NY + y
    entry_barrier(h, z, y)

    def columns(owner, width):
        return pl.ds(pl.multiple_of(owner * width, width), width)

    half = pl.ds(pl.multiple_of(lax.rem(h, 2) * ROWS, ROWS), ROWS)
    mine = pl.ds(pl.multiple_of(h * ROWS, ROWS), ROWS)

    def head_parts(owner):
        return (
            (k_ref.at[:, columns(owner, HEAD_SIZE)], gath.at[0, h // 2, half, pl.ds(0, HEAD_SIZE)]),
            (v_ref.at[:, columns(owner, HEAD_SIZE)], gath.at[0, h // 2, half, pl.ds(HEAD_SIZE, HEAD_SIZE)]),
            (q_ref.at[:, columns(owner, WIDE)], qh_ref.at[mine, :]),
            (do_ref.at[:, columns(owner, WIDE)], doh_ref.at[mine, :]),
            (st_ref.at[owner], sth_ref.at[h]),
        )

    def head_copy(d, part):
        owner = lax.rem(h + d, NH)
        src, dst = head_parts(owner)[part]
        return pltpu.make_async_remote_copy(
            src_ref=src, dst_ref=dst, send_sem=x_send.at[part, d - 1], recv_sem=x_recv.at[part, d - 1],
            device_id={"head": owner}, device_id_type=MESH,
        )

    def own_copy(part):
        src, dst = head_parts(h)[part]
        return pltpu.make_async_copy(src, dst, local.at[part])

    def up_copy(k, c):
        return pltpu.make_async_remote_copy(
            src_ref=gath.at[k, c], dst_ref=gath.at[k + 1, c], send_sem=u_send.at[k, c], recv_sem=u_recv.at[k, c],
            device_id={"ctx": above}, device_id_type=MESH,
        )

    def down_copy(k, c):
        return pltpu.make_async_remote_copy(
            src_ref=gath.at[lax.rem(NZ - k, NZ), c], dst_ref=gath.at[NZ - 1 - k, c],
            send_sem=d_send.at[k, c], recv_sem=d_recv.at[k, c],
            device_id={"ctx": below}, device_id_type=MESH,
        )

    def across_copy(s, dy):
        return pltpu.make_async_remote_copy(
            src_ref=picked.at[s, dy], dst_ref=kv_ref.at[TILES + s * NY + dy],
            send_sem=y_send.at[s, dy - 1], recv_sem=y_recv.at[s, dy - 1],
            device_id={"ctx": z * NY + lax.rem(y + dy, NY)}, device_id_type=MESH,
        )

    def keep_copy(s):
        return pltpu.make_async_copy(picked.at[s, 0], kv_ref.at[TILES + s * NY], out_sem.at[s])

    own_tiles = pltpu.make_async_copy(gath.at[0], kv_ref.at[pl.ds(0, TILES)], out_sem.at[NZ])

    for part in (0, 1):
        for d in range(1, NH):
            head_copy(d, part).start()
        own_copy(part).start()
    make_selection(z, y, lists_ref, sel)
    for part in (0, 1):
        own_copy(part).wait()
        for d in range(1, NH):
            head_copy(d, part).wait_recv()

    def pick(s):
        for dy in range(NY):
            want = sel[dy, pl.ds(s, 1), :]
            for c in range(TILES):
                weight = (want == c).astype(F32).astype(BF16)
                weight = jnp.concatenate([weight, weight], axis=1)
                term = gath[s, c] * weight
                total = term if c == 0 else total + term
            picked[s, dy] = total
            if dy == 0:
                keep_copy(s).start()
            else:
                across_copy(s, dy).start()

    def ring(k, _):
        @pl.loop(0, TILES)
        def _(c):
            @pl.when(k > 0)
            def _():
                up_copy(k - 1, c).wait_recv()

            up_copy(k, c).start()

            @pl.when(k > 0)
            def _():
                down_copy(k - 1, c).wait_recv()

            @pl.when(k < DOWN)
            def _():
                down_copy(k, c).start()

        @pl.when(k == 0)
        def _():
            for part in (2, 3, 4):
                for d in range(1, NH):
                    head_copy(d, part).start()
                own_copy(part).start()
            own_tiles.start()

        pick(k)

        @pl.when(k > 0)
        def _():
            pick(NZ - k)

        return 0

    lax.fori_loop(0, UP, ring, 0)
    for c in range(TILES):
        up_copy(UP - 1, c).wait_recv()
    pick(UP)

    @pl.loop(0, NZ)
    def _(s):
        keep_copy(s).wait()
        for dy in range(1, NY):
            across_copy(s, dy).wait()

    @pl.loop(0, UP)
    def _(k):
        for c in range(TILES):
            up_copy(k, c).wait_send()

    @pl.loop(0, DOWN)
    def _(k):
        for c in range(TILES):
            down_copy(k, c).wait_send()

    own_tiles.wait()
    for part in (0, 1):
        for d in range(1, NH):
            head_copy(d, part).wait_send()
    for part in (2, 3, 4):
        own_copy(part).wait()
        for d in range(1, NH):
            head_copy(d, part).wait()


def pairs_kernel(index_ref, count_ref, q_ref, do_ref, st_ref, kv_ref, dq_ref, own_ref, slot_ref, qs, ds, total, dqt):
    h, z, y = position()
    del h
    node = z * NY + y

    @pl.loop(0, TILES + NZ * NY)
    def _(i):
        total[i] = jnp.zeros((TILE, 2 * HEAD_SIZE), F32)

    order = lax.broadcasted_iota(jnp.int32, (TILE, TILE), 0) - lax.broadcasted_iota(jnp.int32, (TILE, TILE), 1)
    order = jnp.concatenate([order, order], axis=1)
    nt = (((1,), (1,)), ((), ()))
    tn = (((0,), (0,)), ((), ()))

    @pl.loop(0, TILES)
    def _(t):
        rows = pl.ds(pl.multiple_of(t * TILE, TILE), TILE)
        for g in range(GROUP):
            qs[g * TILE : (g + 1) * TILE] = q_ref[rows, g * HEAD_SIZE : (g + 1) * HEAD_SIZE]
            ds[g * TILE : (g + 1) * TILE] = do_ref[rows, g * HEAD_SIZE : (g + 1) * HEAD_SIZE]
        dqt[...] = jnp.zeros_like(dqt)
        stats = st_ref[2 * t] + st_ref[2 * t + 1]
        query_tile = node * TILES + t

        def entry(p, _):
            tile = index_ref[query_tile, p]
            holder = tile // TILES
            slot = lax.rem(z - holder // NY + NZ, NZ) * NY + lax.rem(y - lax.rem(holder, NY) + NY, NY)
            place = jnp.where(holder == node, lax.rem(tile, TILES), TILES + slot)
            limit = jnp.where(tile == query_tile, 0, TILE)
            key = kv_ref[place, :, :HEAD_SIZE]
            value = kv_ref[place, :, HEAD_SIZE:]
            dk = jnp.zeros((TILE, HEAD_SIZE), F32)
            dv = jnp.zeros((TILE, HEAD_SIZE), F32)
            for g in range(0, GROUP, 2):
                span = slice(g * TILE, (g + 2) * TILE)
                norm = jnp.concatenate([stats[g : g + 1], stats[g + 1 : g + 2]], axis=1)
                delta = jnp.concatenate([stats[GROUP + g : GROUP + g + 1], stats[GROUP + g + 1 : GROUP + g + 2]], axis=1)
                q2 = qs[span]
                d2 = ds[span]
                scores = lax.dot_general(key, q2, nt, preferred_element_type=F32)
                weights = jnp.where(order <= limit, jnp.exp2(scores * (SCALE * LOG2E) - norm), 0.0)
                dp = lax.dot_general(value, d2, nt, preferred_element_type=F32)
                score_grad = (weights * (dp - delta)).astype(BF16)
                dv += jnp.dot(weights.astype(BF16), d2, preferred_element_type=F32)
                dk += jnp.dot(score_grad, q2, preferred_element_type=F32)
                dqt[:, span] += lax.dot_general(key, score_grad, tn, preferred_element_type=F32)
            total[place, :, :HEAD_SIZE] += dk
            total[place, :, HEAD_SIZE:] += dv
            return 0

        lax.fori_loop(0, count_ref[query_tile], entry, 0)
        for g in range(GROUP):
            part = dqt[:, g * TILE : (g + 1) * TILE] * SCALE
            dq_ref[rows, g * HEAD_SIZE : (g + 1) * HEAD_SIZE] = part.T.astype(BF16)

    for c in range(TILES):
        own_ref[c, :, :HEAD_SIZE] = total[c, :, :HEAD_SIZE] * SCALE
        own_ref[c, :, HEAD_SIZE:] = total[c, :, HEAD_SIZE:]

    @pl.loop(0, NZ * NY)
    def _(i):
        slot_ref[i, :, :HEAD_SIZE] = (total[TILES + i, :, :HEAD_SIZE] * SCALE).astype(BF16)
        slot_ref[i, :, HEAD_SIZE:] = total[TILES + i, :, HEAD_SIZE:].astype(BF16)


def backward_kernel(
    dq_ref, own_ref, slot_ref, lists_ref,
    gq_ref, gk_ref, gv_ref,
    across, up_out, up_in, down_out, down_in, done, sel,
    x_send, x_recv, local, u_send, u_recv, d_send, d_recv, y_send, y_recv,
):
    h, z, y = position()
    above = lax.rem(z + 1, NZ) * NY + y
    below = lax.rem(z + NZ - 1, NZ) * NY + y
    entry_barrier(h, z, y)

    def columns(owner, width):
        return pl.ds(pl.multiple_of(owner * width, width), width)

    def head_parts(owner):
        half = pl.ds(pl.multiple_of(lax.rem(owner, 2) * ROWS, ROWS), ROWS)
        rows = pl.ds(pl.multiple_of(owner * ROWS, ROWS), ROWS)
        return (
            (dq_ref.at[rows, :], gq_ref.at[:, columns(h, WIDE)]),
            (done.at[owner // 2, half, pl.ds(0, HEAD_SIZE)], gk_ref.at[:, columns(h, HEAD_SIZE)]),
            (done.at[owner // 2, half, pl.ds(HEAD_SIZE, HEAD_SIZE)], gv_ref.at[:, columns(h, HEAD_SIZE)]),
        )

    def head_copy(d, part):
        owner = lax.rem(h + d, NH)
        src, dst = head_parts(owner)[part]
        return pltpu.make_async_remote_copy(
            src_ref=src, dst_ref=dst, send_sem=x_send.at[part, d - 1], recv_sem=x_recv.at[part, d - 1],
            device_id={"head": owner}, device_id_type=MESH,
        )

    def own_copy(part):
        src, dst = head_parts(h)[part]
        return pltpu.make_async_copy(src, dst, local.at[part])

    def across_copy(s, dy):
        return pltpu.make_async_remote_copy(
            src_ref=slot_ref.at[s * NY + dy], dst_ref=across.at[s, dy - 1],
            send_sem=y_send.at[s, dy - 1], recv_sem=y_recv.at[s, dy - 1],
            device_id={"ctx": z * NY + lax.rem(y + NY - dy, NY)}, device_id_type=MESH,
        )

    def down_copy(k, c):
        return pltpu.make_async_remote_copy(
            src_ref=down_out.at[k, c], dst_ref=down_in.at[k, c], send_sem=d_send.at[k, c], recv_sem=d_recv.at[k, c],
            device_id={"ctx": below}, device_id_type=MESH,
        )

    def up_copy(k, c):
        return pltpu.make_async_remote_copy(
            src_ref=up_out.at[k, c], dst_ref=up_in.at[k, c], send_sem=u_send.at[k, c], recv_sem=u_recv.at[k, c],
            device_id={"ctx": above}, device_id_type=MESH,
        )

    def send_across(s):
        for dy in range(1, NY):
            across_copy(s, dy).start()

    @pl.loop(0, UP)
    def _(k):
        send_across(UP - k)

        @pl.when(k < DOWN)
        def _():
            send_across(UP + 1 + k)

    send_across(0)
    for d in range(1, NH):
        head_copy(d, 0).start()
    own_copy(0).start()
    make_selection(z, y, lists_ref, sel)

    def wait_across(s):
        for dy in range(1, NY):
            across_copy(s, dy).wait_recv()

    def asked(s, c, first):
        total = None
        for dy in range(first, NY):
            want = sel[dy, pl.ds(s, 1), :]
            weight = (want == c).astype(F32)
            weight = jnp.concatenate([weight, weight], axis=1)
            block = slot_ref[s * NY] if dy == 0 else across[s, dy - 1]
            term = block.astype(F32) * weight
            total = term if total is None else total + term
        return total

    def ring(k, _):
        wait_across(UP - k)

        @pl.when(k < DOWN)
        def _():
            wait_across(UP + 1 + k)

        @pl.loop(0, TILES)
        def _(c):
            part = asked(UP - k, c, 0)

            @pl.when(k == 0)
            def _():
                down_out[k, c] = part.astype(BF16)

            @pl.when(k > 0)
            def _():
                down_copy(k - 1, c).wait_recv()
                down_out[k, c] = (part + down_in[k - 1, c].astype(F32)).astype(BF16)

            down_copy(k, c).start()

            @pl.when(k < DOWN)
            def _():
                other = asked(UP + 1 + k, c, 0)

                @pl.when(k == 0)
                def _():
                    up_out[k, c] = other.astype(BF16)

                @pl.when(k > 0)
                def _():
                    up_copy(k - 1, c).wait_recv()
                    up_out[k, c] = (other + up_in[k - 1, c].astype(F32)).astype(BF16)

                up_copy(k, c).start()

        return 0

    lax.fori_loop(0, UP, ring, 0)
    wait_across(0)

    @pl.loop(0, TILES)
    def _(c):
        part = own_ref[c] + asked(0, c, 1)
        up_copy(DOWN - 1, c).wait_recv()
        part += up_in[DOWN - 1, c].astype(F32)
        down_copy(UP - 1, c).wait_recv()
        done[c] = (part + down_in[UP - 1, c].astype(F32)).astype(BF16)

    for part in (1, 2):
        for d in range(1, NH):
            head_copy(d, part).start()
        own_copy(part).start()

    @pl.loop(0, NZ)
    def _(s):
        for dy in range(1, NY):
            across_copy(s, dy).wait_send()

    @pl.loop(0, UP)
    def _(k):
        for c in range(TILES):
            down_copy(k, c).wait_send()

    @pl.loop(0, DOWN)
    def _(k):
        for c in range(TILES):
            up_copy(k, c).wait_send()

    for part in (0, 1, 2):
        own_copy(part).wait()
        for d in range(1, NH):
            head_copy(d, part).wait()


def any_spec():
    return pl.BlockSpec(memory_space=pl.ANY)


def vmem_spec():
    return pl.BlockSpec(memory_space=pltpu.VMEM)


def smem_spec():
    return pl.BlockSpec(memory_space=pltpu.SMEM)


def shape(dims, dtype):
    return jax.ShapeDtypeStruct(dims, dtype)


def on_device(queries, outputs, output_gradient, keys, values, log_row_norm, kv_index, counts):
    dma = pltpu.SemaphoreType.DMA
    delta = jnp.sum(
        (output_gradient.astype(F32) * outputs.astype(F32)).reshape(ROWS, QUERY_HEADS, HEAD_SIZE), axis=2
    )
    stats = jnp.concatenate(
        [(log_row_norm * LOG2E).T.reshape(NH, GROUP, ROWS), delta.T.reshape(NH, GROUP, ROWS)], axis=1
    )
    odd = lax.rem(lax.axis_index("head"), 2) == 1
    stats = jnp.concatenate([jnp.where(odd, 0.0, stats), jnp.where(odd, stats, 0.0)], axis=2)
    listed = jnp.arange(kv_index.shape[1], dtype=jnp.int32)[None, :] < counts[:, None]
    lists = jnp.where(listed, kv_index, -1).reshape(NZ * NY, -1)
    lists = jnp.pad(lists, ((0, 0), (0, 128 - lists.shape[1])), constant_values=-1)

    tile_pair = (TILE, 2 * HEAD_SIZE)
    qh, doh, sth, kv = pl.pallas_call(
        forward_kernel,
        out_shape=(
            shape((NH * ROWS, WIDE), BF16),
            shape((NH * ROWS, WIDE), BF16),
            shape((NH, 2 * GROUP, 128), F32),
            shape((TILES + NZ * NY,) + tile_pair, BF16),
        ),
        in_specs=[any_spec()] * 5 + [vmem_spec()],
        out_specs=(any_spec(),) * 4,
        scratch_shapes=[
            pltpu.VMEM((NZ, TILES) + tile_pair, BF16),
            pltpu.VMEM((NZ, NY) + tile_pair, BF16),
            pltpu.VMEM((NY, NZ, 128), jnp.int32),
            dma((5, NH - 1)), dma((5, NH - 1)), dma((5,)),
            dma((UP, TILES)), dma((UP, TILES)), dma((DOWN, TILES)), dma((DOWN, TILES)),
            dma((NZ, NY - 1)), dma((NZ, NY - 1)), dma((NZ + 1,)),
        ],
        compiler_params=pltpu.CompilerParams(collective_id=0, has_side_effects=True, vmem_limit_bytes=24 << 20),
        name="exchange_in",
    )(queries, output_gradient, keys, values, stats, lists)

    dq, own, slots = pl.pallas_call(
        pairs_kernel,
        out_shape=(
            shape((NH * ROWS, WIDE), BF16),
            shape((TILES,) + tile_pair, F32),
            shape((NZ * NY,) + tile_pair, BF16),
        ),
        in_specs=[smem_spec()] * 2 + [vmem_spec()] * 4,
        out_specs=(vmem_spec(),) * 3,
        scratch_shapes=[
            pltpu.VMEM((GROUP * TILE, HEAD_SIZE), BF16),
            pltpu.VMEM((GROUP * TILE, HEAD_SIZE), BF16),
            pltpu.VMEM((TILES + NZ * NY,) + tile_pair, F32),
            pltpu.VMEM((HEAD_SIZE, GROUP * TILE), F32),
        ],
        compiler_params=pltpu.CompilerParams(vmem_limit_bytes=48 << 20),
        name="pairs",
    )(kv_index, counts, qh, doh, sth, kv)

    return pl.pallas_call(
        backward_kernel,
        out_shape=(
            shape((ROWS, NH * WIDE), BF16),
            shape((ROWS, NH * HEAD_SIZE), BF16),
            shape((ROWS, NH * HEAD_SIZE), BF16),
        ),
        in_specs=[any_spec(), vmem_spec(), vmem_spec(), vmem_spec()],
        out_specs=(any_spec(),) * 3,
        scratch_shapes=[
            pltpu.VMEM((NZ, NY - 1) + tile_pair, BF16),
            pltpu.VMEM((DOWN, TILES) + tile_pair, BF16),
            pltpu.VMEM((DOWN, TILES) + tile_pair, BF16),
            pltpu.VMEM((UP, TILES) + tile_pair, BF16),
            pltpu.VMEM((UP, TILES) + tile_pair, BF16),
            pltpu.VMEM((TILES,) + tile_pair, BF16),
            pltpu.VMEM((NY, NZ, 128), jnp.int32),
            dma((3, NH - 1)), dma((3, NH - 1)), dma((3,)),
            dma((DOWN, TILES)), dma((DOWN, TILES)), dma((UP, TILES)), dma((UP, TILES)),
            dma((NZ, NY - 1)), dma((NZ, NY - 1)),
        ],
        compiler_params=pltpu.CompilerParams(collective_id=1, has_side_effects=True, vmem_limit_bytes=40 << 20),
        name="exchange_out",
    )(dq, own, slots, lists)


def solution(mesh):
    rows = P(("ctx", "head"), None)
    return jax.shard_map(
        on_device,
        mesh=mesh,
        in_specs=(rows,) * 6 + (P(), P()),
        out_specs=(rows,) * 3,
        check_vma=False,
    )
```

time: 1280 us -> 195 us (0.15)
  waiting for transfers between devices: 580 us -> 0 us
  starting transfers between devices: 526 us -> 0 us
  Pallas kernels: 0 us -> 179 us
  local copies, waits for them, and re-layouts: 71.2 us -> 9.42 us
  loops' own time: 33.8 us -> 0 us
  matrix products: 30.3 us -> 0 us
  other arithmetic: 30.4 us -> 5.69 us
    all_to_all x11 -> x0, waiting for transfers between devices: 580 us -> none  [the longest x1 357 us: on_device(): lax.all_to_all(status[1][tiles:tiles + ctx_count], 'ctx', split_axis=0, c...]
    all_to_all x11 -> x0, starting transfers between devices: 526 us -> none  [the longest x1 456 us: on_device(): lax.all_to_all(status[1][tiles:tiles + ctx_count], 'ctx', split_axis=0, c...]
    pallas_call x0 -> x3, Pallas kernels: none -> 179 us  [the longest x1 91.2 us: on_device(): pl.pallas_call(backward_kernel, out_shape=(shape((ROWS, NH * WIDE), BF16)...]
    another operation x4 -> x0, loops' own time: 33.8 us -> none  [on_device(): status = lax.fori_loop(0, counts[query_tile], entry, status)]
    dot_general x37 -> x0, matrix products: 30.3 us -> none  [the longest x7 8.59 us: pairwise_terms(): jnp.einsum('agqk,qagd->kad', score_grad, query_row_block, preferred_eleme...]
    scatter-add x7 -> x0, other arithmetic: 15.3 us -> none  [entry(): pair_sums.at[place].add(pairwise_gradient)]
  transfers between devices with their start and end apart: 11 -> 0, of which waited for: 10 -> 0; matrix products, arithmetic and copies ran while one was open for 4% -> 0% of each run, Pallas kernels for 0% -> 0%
where the time goes in v1:
time: 195 us
  Pallas kernels  179 us (92%)
  local copies, waits for them, and re-layouts  9.42 us (5%)
  other arithmetic  5.69 us (3%)
    pallas_call x1, Pallas kernels, on_device(): pl.pallas_call(backward_kernel, out_shape=(shape((ROWS, NH * WIDE), BF16)...  91.2 us
    pallas_call x1, Pallas kernels, on_device(): pl.pallas_call(forward_kernel, out_shape=(shape((NH * ROWS, WIDE), BF16),...  73.9 us
    pallas_call x1, Pallas kernels, on_device(): pl.pallas_call(pairs_kernel, out_shape=(shape((NH * ROWS, WIDE), BF16), s...  14.1 us
    unnamed x19, local copies, waits for them, and re-layouts  9.06 us

profile of v1, /device:TPU:1, one launch (start us, length us, event | category | flops | bytes accessed | tf_op | source)
XLA Modules:
  0.0 195.1 jit_solution(17592310332315665966)
XLA Ops:
  0.6 0.7 fusion.2
  1.4 0.8 multiply_bitcast_fusion.1
  2.1 0.1 copy.17
  2.2 0.1 copy.19
  2.3 0.1 reshape.22
  2.4 0.8 copy.20.index_ref
  3.3 1.7 multiply_bitcast_fusion
  5.0 1.7 copy.21
  6.7 0.0 copy-start.2
  6.7 0.0 copy-start.3
  6.7 0.0 copy-start.4
  6.7 0.0 copy-start.5
  6.7 0.0 copy-start.6
  6.8 2.4 %reduce_sum.9 = f32[64,64]{1,0:T(8,128)S(1)} reduce(f32[64,64,128]{2,1,0:T(8,128)} %bitcast.8, f32[]{:T(128)} %constant.15.clone.1), dimensions={2}, to_apply=%region_0.0 | reduce | flops 520192 | bytes 2113540 | tf_op jit(solution)/shard_map/reduce_sum | solution.py:460
  9.1 0.1 copy.18
  9.2 0.1 pad_maximum_fusion.1.st_ref
  9.3 0.0 copy-done.2
  9.3 0.0 copy-done.3
  9.3 0.0 copy-done.4
  9.3 0.0 copy-done.5
  9.3 73.9 %exchange_in.1 = (bf16[512,1024]{1,0:T(8,128)(2,1)S(1)}, bf16[512,1024]{1,0:T(8,128)(2,1)S(1)}, f32[8,16,128]{2,1,0:T(8,128)S(1)}, bf16[68,128,256]{2,1,0:T(8,128)(2,1)S(1)}) custom-call(bf16[64,8192]{1,0:T(8,128)(2,1)S(1)} %copy-done.3, bf16[64,8192]{1,0:T(8,128)(2,1)S(1)} %copy-done.2, bf16[64,1024]{1,0:T(8,128)(2,1)S(1)} %copy-done.4, ...), custom_call_target="tpu_custom_call" | custom-call | tf_op jit(solution)/shard_map/exchange_in/pallas_call | solution.py:473
  83.3 0.0 copy-start
  83.3 2.0 %copy-done = bf16[68,128,256]{2,1,0:T(8,128)(2,1)} copy-done((bf16[68,128,256]{2,1,0:T(8,128)(2,1)}, bf16[68,128,256]{2,1,0:T(8,128)(2,1)S(1)}, u32[]{:S(2)}) %copy-start) | copy-done | bytes 4456472
  85.3 0.0 copy-done.6
  85.3 14.1 %pairs.1 = (bf16[512,1024]{1,0:T(8,128)(2,1)S(1)}, f32[4,128,256]{2,1,0:T(8,128)S(1)}, bf16[64,128,256]{2,1,0:T(8,128)(2,1)}) custom-call(s32[256,10]{1,0:T(8,128)S(1)} %copy.20.index_ref, s32[256]{0:T(256)S(1)} %copy-done.6, bf16[512,1024]{1,0:T(8,128)(2,1)S(1)} %get-tuple-element.10.q_ref, bf16[512,1024]{1,0:T(8,128)(2,1)S(1)} %get-tuple-element.11.do_ref, ...), custom_call_target="tpu_custom_call" | custom-call | tf_op jit(solution)/shard_map/pairs/pallas_call | solution.py:495
  99.4 0.0 copy-start.1
  99.4 2.2 %copy-done.1 = bf16[64,128,256]{2,1,0:T(8,128)(2,1)S(1)} copy-done((bf16[64,128,256]{2,1,0:T(8,128)(2,1)S(1)}, bf16[64,128,256]{2,1,0:T(8,128)(2,1)}, u32[]{:S(2)}) %copy-start.1) | copy-done | bytes 4194328
  101.6 91.2 %exchange_out.1 = (bf16[64,8192]{1,0:T(8,128)(2,1)S(1)}, bf16[64,1024]{1,0:T(8,128)(2,1)S(1)}, bf16[64,1024]{1,0:T(8,128)(2,1)S(1)}) custom-call(bf16[512,1024]{1,0:T(8,128)(2,1)S(1)} %get-tuple-element.14.dq_ref, f32[4,128,256]{2,1,0:T(8,128)S(1)} %get-tuple-element.15.own_ref, bf16[64,128,256]{2,1,0:T(8,128)(2,1)S(1)} %copy-done.1, s32[64,128]{1,0:T(8,128)S(1)} %pad.4.lists_ref), custom_call_target="tpu_custom_call" | custom-call | tf_op jit(solution)/shard_map/exchange_out/pallas_call | solution.py:514
  192.8 1.0 copy.25
  193.8 0.7 copy.26
  194.4 0.7 copy.27
  (2 shorter events, 0.0 us)
Async XLA Ops:
  6.7 2.6 %copy-start.2 = (bf16[64,8192]{1,0:T(8,128)(2,1)S(1)}, bf16[64,8192]{1,0:T(8,128)(2,1)}, u32[]{:S(2)}) copy-start(bf16[64,8192]{1,0:T(8,128)(2,1)} %do_ref.1) | copy-start | bytes 3145732
  6.7 2.6 %copy-start.3 = (bf16[64,8192]{1,0:T(8,128)(2,1)S(1)}, bf16[64,8192]{1,0:T(8,128)(2,1)}, u32[]{:S(2)}) copy-start(bf16[64,8192]{1,0:T(8,128)(2,1)} %q_ref.1) | copy-start | bytes 3145732
  6.7 2.6 %copy-start.4 = (bf16[64,1024]{1,0:T(8,128)(2,1)S(1)}, bf16[64,1024]{1,0:T(8,128)(2,1)}, u32[]{:S(2)}) copy-start(bf16[64,1024]{1,0:T(8,128)(2,1)} %k_ref.1) | copy-start | bytes 393220
  6.7 2.6 %copy-start.5 = (bf16[64,1024]{1,0:T(8,128)(2,1)S(1)}, bf16[64,1024]{1,0:T(8,128)(2,1)}, u32[]{:S(2)}) copy-start(bf16[64,1024]{1,0:T(8,128)(2,1)} %v_ref.1) | copy-start | bytes 393220
  6.7 78.6 %copy-start.6 = (s32[256]{0:T(256)S(1)}, s32[256]{0:T(256)}, u32[]{:S(2)}) copy-start(s32[256]{0:T(256)} %count_ref.1) | copy-start | bytes 3076
  83.3 2.0 %copy-start = (bf16[68,128,256]{2,1,0:T(8,128)(2,1)}, bf16[68,128,256]{2,1,0:T(8,128)(2,1)S(1)}, u32[]{:S(2)}) copy-start(bf16[68,128,256]{2,1,0:T(8,128)(2,1)S(1)} %get-tuple-element.13.kv_ref) | copy-start | bytes 13369348
  99.4 2.2 %copy-start.1 = (bf16[64,128,256]{2,1,0:T(8,128)(2,1)S(1)}, bf16[64,128,256]{2,1,0:T(8,128)(2,1)}, u32[]{:S(2)}) copy-start(bf16[64,128,256]{2,1,0:T(8,128)(2,1)} %get-tuple-element.16.slot_ref) | copy-start | bytes 12582916

commit v2 on v0

v2 whole, which is shorter than its diff:
```python
import math

import jax
import jax.numpy as jnp
from jax import lax
from jax.experimental import pallas as pl
from jax.experimental.pallas import tpu as pltpu
from jax.sharding import PartitionSpec as P

QUERY_HEADS = 64
KEY_VALUE_HEADS = 8
HEAD_SIZE = 128
TILE = 128
GROUP = QUERY_HEADS // KEY_VALUE_HEADS
TILES = 4
ENTRIES = 10
PAIRS = TILES * ENTRIES
NZ = 16
NY = 4
NH = 8
HOPS = NZ // 2
CHUNK = TILES // 2
ROWS = 64
WIDE = GROUP * HEAD_SIZE
PLACES = TILES + NZ * NY
SCALE = HEAD_SIZE ** (-0.5)
LOG2E = math.log2(math.e)
MESH = pl.DeviceIdType.MESH
F32 = jnp.float32
BF16 = jnp.bfloat16
NT = (((1,), (1,)), ((), ()))
TN = (((0,), (0,)), ((), ()))

K, V, Q, DO, ST, GQ, GV, GK = range(8)


def kernel(
    q_ref, o_ref, do_ref, k_ref, v_ref, norm_ref, lists_ref, meta_ref,
    gq_ref, gk_ref, gv_ref,
    k_ring, v_ring, k_all, v_all, picked, q_all, do_all, o_own, do_own, norm_t, st_out, st_all, sel,
    weights, dv_pairs, dk_pairs, dq_t, dq_out, terms, dv_across, dk_across, down_out, up_out,
    dv_down, dv_up, dk_down, dk_up, dv_done, dk_done,
    x_send, x_recv, local, own_sem,
    u_send, u_recv, d_send, d_recv, y_send, y_recv,
    bu_send, bu_recv, bd_send, bd_recv, by_send, by_recv,
):
    ctx = lax.axis_index("ctx")
    h, z, y = lax.axis_index("head"), ctx // NY, lax.rem(ctx, NY)
    above = lax.rem(z + 1, NZ) * NY + y
    below = lax.rem(z + NZ - 1, NZ) * NY + y

    barrier = pltpu.get_barrier_semaphore()

    def greet(**where):
        pl.semaphore_signal(barrier, inc=1, device_id=where, device_id_type=MESH)

    for d in range(1, NH):
        greet(head=lax.rem(h + d, NH))
    for d in range(1, NY):
        greet(ctx=z * NY + lax.rem(y + d, NY))
    greet(ctx=above)
    greet(ctx=below)

    own_load = [
        pltpu.make_async_copy(o_ref, o_own, own_sem.at[0]),
        pltpu.make_async_copy(do_ref, do_own, own_sem.at[1]),
    ]
    for copy in own_load:
        copy.start()
    pl.semaphore_wait(barrier, NH + NY)

    def columns(owner, width):
        return pl.ds(pl.multiple_of(owner * width, width), width)

    def half(owner):
        return pl.ds(pl.multiple_of(lax.rem(owner, 2) * ROWS, ROWS), ROWS)

    def rows_of(owner):
        return pl.ds(pl.multiple_of(owner * ROWS, ROWS), ROWS)

    def head_ends(part, owner, d):
        if part == K:
            return k_ref.at[:, columns(owner, HEAD_SIZE)], k_ring.at[0, h // 2, half(h), :]
        if part == V:
            return v_ref.at[:, columns(owner, HEAD_SIZE)], v_ring.at[0, h // 2, half(h), :]
        if part == Q:
            return q_ref.at[:, columns(owner, WIDE)], q_all.at[rows_of(h), :]
        if part == DO:
            return do_ref.at[:, columns(owner, WIDE)], do_all.at[rows_of(h), :]
        if part == ST:
            return st_out.at[d], st_all.at[h]
        if part == GQ:
            return dq_out.at[rows_of(owner), :], gq_ref.at[:, columns(h, WIDE)]
        if part == GV:
            return dv_done.at[owner // 2, half(owner), :], gv_ref.at[:, columns(h, HEAD_SIZE)]
        return dk_done.at[owner // 2, half(owner), :], gk_ref.at[:, columns(h, HEAD_SIZE)]

    def head_copy(part, d):
        owner = lax.rem(h + d, NH)
        src, dst = head_ends(part, owner, d)
        return pltpu.make_async_remote_copy(
            src_ref=src, dst_ref=dst, send_sem=x_send.at[part, d - 1], recv_sem=x_recv.at[part, d - 1],
            device_id={"head": owner}, device_id_type=MESH,
        )

    def own_copy(part):
        src, dst = head_ends(part, h, 0)
        return pltpu.make_async_copy(src, dst, local.at[part])

    def head_start(part):
        for d in range(1, NH):
            head_copy(part, d).start()
        own_copy(part).start()

    def head_arrived(part):
        own_copy(part).wait()
        for d in range(1, NH):
            head_copy(part, d).wait_recv()

    def head_sent(part):
        for d in range(1, NH):
            head_copy(part, d).wait_send()

    ring_of, all_of = (k_ring, v_ring), (k_all, v_all)

    def tiles(c):
        return pl.ds(c * CHUNK, CHUNK)

    def up_copy(w, j, c):
        ring = ring_of[w]
        return pltpu.make_async_remote_copy(
            src_ref=ring.at[j, tiles(c)], dst_ref=ring.at[j + 1, tiles(c)],
            send_sem=u_send.at[w, j, c], recv_sem=u_recv.at[w, j, c],
            device_id={"ctx": above}, device_id_type=MESH,
        )

    def down_copy(w, j, c):
        ring = ring_of[w]
        return pltpu.make_async_remote_copy(
            src_ref=ring.at[lax.rem(NZ - j, NZ), tiles(c)], dst_ref=ring.at[NZ - 1 - j, tiles(c)],
            send_sem=d_send.at[w, j, c], recv_sem=d_recv.at[w, j, c],
            device_id={"ctx": below}, device_id_type=MESH,
        )

    def across_copy(w, s, dy):
        return pltpu.make_async_remote_copy(
            src_ref=picked.at[w, s, dy - 1], dst_ref=all_of[w].at[TILES + s * NY + dy],
            send_sem=y_send.at[w, s, dy - 1], recv_sem=y_recv.at[w, s, dy - 1],
            device_id={"ctx": z * NY + lax.rem(y + dy, NY)}, device_id_type=MESH,
        )

    def pick(w, s):
        ring = ring_of[w]
        for dy in range(NY):
            want = sel[dy, pl.ds(s, 1), :]
            for c in range(TILES):
                term = ring[s, c] * (want == c).astype(F32).astype(BF16)
                total = term if c == 0 else total + term
            if dy == 0:
                all_of[w][TILES + s * NY] = total
            else:
                picked[w, s, dy - 1] = total
                across_copy(w, s, dy).start()

    def gather(w, beside):
        def step(j, _):
            for c in range(2):

                @pl.when(j > 0)
                def _():
                    up_copy(w, j - 1, c).wait_recv()

                if c == 0:
                    up_copy(w, j, c).start()
                else:

                    @pl.when(j < HOPS - 1)
                    def _():
                        up_copy(w, j, c).start()

                @pl.when(j > 0)
                def _():
                    down_copy(w, j - 1, c).wait_recv()

                if c == 1:
                    down_copy(w, j, c).start()
                else:

                    @pl.when(j < HOPS - 1)
                    def _():
                        down_copy(w, j, c).start()

                if c == 1:
                    pick(w, j)

                    @pl.when(j > 0)
                    def _():
                        pick(w, NZ - j)

                beside(j, c)
            return 0

        lax.fori_loop(0, HOPS, step, 0)

    def gather_end(w):
        up_copy(w, HOPS - 1, 0).wait_recv()
        down_copy(w, HOPS - 1, 1).wait_recv()
        pick(w, HOPS)

    def gathered(w):
        @pl.loop(0, NZ)
        def _(s):
            for dy in range(1, NY):
                across_copy(w, s, dy).wait_recv()

    order = lax.broadcasted_iota(jnp.int32, (TILE, TILE), 0) - lax.broadcasted_iota(jnp.int32, (TILE, TILE), 1)
    order = jnp.concatenate([order, order], axis=1)

    def two_heads(ref, t, g):
        rows = pl.ds(pl.multiple_of(t * TILE, TILE), TILE)
        return jnp.concatenate(
            [ref[rows, g * HEAD_SIZE : (g + 1) * HEAD_SIZE], ref[rows, (g + 1) * HEAD_SIZE : (g + 2) * HEAD_SIZE]],
            axis=0,
        )

    def stat_rows(t, g):
        both = st_all[2 * t] + st_all[2 * t + 1]
        return jnp.concatenate([both[g : g + 1], both[g + 1 : g + 2]], axis=1)

    def first_half(e):
        t = e // ENTRIES
        key = k_all[meta_ref[0, e]]
        limit = meta_ref[0, PAIRS + e]
        dv = jnp.zeros((TILE, HEAD_SIZE), F32)
        for g in range(0, GROUP, 2):
            scores = lax.dot_general(key, two_heads(q_all, t, g), NT, preferred_element_type=F32)
            part = jnp.where(order <= limit, jnp.exp2(scores * (SCALE * LOG2E) - stat_rows(t, g)), 0.0)
            weights[e, :, g * TILE : (g + 2) * TILE] = part
            dv += jnp.dot(part.astype(BF16), two_heads(do_all, t, g), preferred_element_type=F32)
        dv_pairs[e] = dv

    def second_half(e):
        t = e // ENTRIES
        place = meta_ref[0, e]
        key = k_all[place]
        value = v_all[place]
        dk = jnp.zeros((TILE, HEAD_SIZE), F32)
        for g in range(0, GROUP, 2):
            span = slice(g * TILE, (g + 2) * TILE)
            dp = lax.dot_general(value, two_heads(do_all, t, g), NT, preferred_element_type=F32)
            score_grad = (weights[e, :, span] * (dp - stat_rows(t, GROUP + g))).astype(BF16)
            dk += jnp.dot(score_grad, two_heads(q_all, t, g), preferred_element_type=F32)
            dq_t[t, :, span] += lax.dot_general(key, score_grad, TN, preferred_element_type=F32)
        dk_pairs[e] = dk * SCALE

    pairs_of, cross_of, done_of = (dk_pairs, dv_pairs), (dk_across, dv_across), (dk_done, dv_done)
    down_of, up_of = (dk_down, dv_down), (dk_up, dv_up)

    def cross_back(w, s, dy):
        return pltpu.make_async_remote_copy(
            src_ref=terms.at[w, s, dy], dst_ref=cross_of[w].at[s, dy - 1],
            send_sem=by_send.at[w, s, dy - 1], recv_sem=by_recv.at[w, s, dy - 1],
            device_id={"ctx": z * NY + lax.rem(y + NY - dy, NY)}, device_id_type=MESH,
        )

    def down_back(w, j, c):
        return pltpu.make_async_remote_copy(
            src_ref=down_out.at[w, j, tiles(c)], dst_ref=down_of[w].at[j, tiles(c)],
            send_sem=bd_send.at[w, j, c], recv_sem=bd_recv.at[w, j, c],
            device_id={"ctx": below}, device_id_type=MESH,
        )

    def up_back(w, j, c):
        return pltpu.make_async_remote_copy(
            src_ref=up_out.at[w, j, tiles(c)], dst_ref=up_of[w].at[j, tiles(c)],
            send_sem=bu_send.at[w, j, c], recv_sem=bu_recv.at[w, j, c],
            device_id={"ctx": above}, device_id_type=MESH,
        )

    def place_sum(w, place):
        for t in range(TILES):
            term = pairs_of[w][meta_ref[0, 2 * PAIRS + t * PLACES + place]]
            total = term if t == 0 else total + term
        return total

    def give(w, s):
        for dy in range(NY):
            terms[w, s, dy] = place_sum(w, TILES + s * NY + dy).astype(BF16)
            if dy > 0:
                cross_back(w, s, dy).start()

    def taken(w, s):
        for dy in range(1, NY):
            cross_back(w, s, dy).wait_recv()

    def asked(w, s, c, first):
        total = None
        for dy in range(first, NY):
            weight = (sel[dy, pl.ds(s, 1), :] == c).astype(F32)
            block = terms[w, s, 0] if dy == 0 else cross_of[w][s, dy - 1]
            term = block.astype(F32) * weight
            total = term if total is None else total + term
        return total

    def reduce_start(w):
        for s in (8, 7, 9, 6, 10):
            give(w, s)
        for c in range(CHUNK):
            down_of[w][0, CHUNK + c] = jnp.zeros((TILE, HEAD_SIZE), BF16)
            up_of[w][0, c] = jnp.zeros((TILE, HEAD_SIZE), BF16)

    def hop(w, j, c, out, into, slot, copy, first):
        if c == first:

            @pl.when(j == 0)
            def _():
                for i in range(c * CHUNK, (c + 1) * CHUNK):
                    out[w, 0, i] = asked(w, HOPS, i, 0).astype(BF16)
                copy(w, j, c).start()

            @pl.when(j > 0)
            def _():
                copy(w, j - 1, c).wait_recv()

        else:

            @pl.when(j > 1)
            def _():
                copy(w, j - 1, c).wait_recv()

        @pl.when(j > 0)
        def _():
            for i in range(c * CHUNK, (c + 1) * CHUNK):
                out[w, j, i] = (asked(w, slot, i, 0) + into[j - 1, i].astype(F32)).astype(BF16)
            copy(w, j, c).start()

    def reduce_ring(w, beside):
        def step(j, _):
            taken(w, HOPS - j)

            @pl.when(j > 0)
            def _():
                taken(w, HOPS + j)

            for c in range(2):
                hop(w, j, c, down_out, down_of[w], HOPS - j, down_back, 0)
                hop(w, j, c, up_out, up_of[w], HOPS + j, up_back, 1)
                if c == 1:

                    @pl.when(j < HOPS - 2)
                    def _():
                        give(w, HOPS - 3 - j)

                    @pl.when(j < HOPS - 3)
                    def _():
                        give(w, HOPS + 3 + j)

                beside(j, c)
            return 0

        lax.fori_loop(0, HOPS, step, 0)

    def reduce_end(w):
        taken(w, 0)
        for i in range(TILES):
            c = i // CHUNK
            part = place_sum(w, i) + asked(w, 0, i, 1)
            if i % CHUNK == 0:
                down_back(w, HOPS - 1, c).wait_recv()
                up_back(w, HOPS - 1, c).wait_recv()
            part += down_of[w][HOPS - 1, i].astype(F32)
            part += up_of[w][HOPS - 1, i].astype(F32)
            done_of[w][i] = part.astype(BF16)

    head_start(K)
    head_start(V)
    slot = lax.broadcasted_iota(jnp.int32, (NZ, 128), 0)
    plane = lax.rem(z - slot + NZ, NZ)
    for dy in range(NY):
        node = z * NY + lax.rem(y + dy, NY)
        entries = lists_ref[pl.ds(node, 1), :]
        match = (entries >> 2) == plane * NY + y
        found = jnp.max(jnp.where(match, entries & 3, -1), axis=1, keepdims=True)
        sel[dy] = jnp.broadcast_to(found, (NZ, 128))
    head_arrived(K)

    lane = lax.broadcasted_iota(jnp.int32, (ROWS, 128), 1)
    keep = (lax.broadcasted_iota(jnp.int32, (GROUP, 128), 1) >= ROWS) == (lax.rem(h, 2) == 1)

    def beside_keys(j, c):
        if c == 0:

            @pl.when(j == 0)
            def _():
                head_start(Q)
                head_start(DO)

        else:

            @pl.when(j == 0)
            def _():
                for copy in own_load:
                    copy.wait()
                block = jnp.concatenate([norm_ref[...], jnp.zeros((ROWS, ROWS), F32)], axis=1) * LOG2E
                norm_t[...] = jnp.concatenate([block, block], axis=0).T
                for i in range(TILES):
                    k_all[i] = k_ring[0, i]
                    dq_t[i] = jnp.zeros((HEAD_SIZE, GROUP * TILE), F32)
                dv_pairs[PAIRS] = jnp.zeros((TILE, HEAD_SIZE), F32)
                dk_pairs[PAIRS] = jnp.zeros((TILE, HEAD_SIZE), F32)

            owner = lax.rem(h + j, NH)
            cols = columns(owner, WIDE)
            product = do_own[:, cols].astype(F32) * o_own[:, cols].astype(F32)
            block = jnp.zeros((ROWS, 128), F32)
            for g in range(GROUP):
                delta = jnp.sum(product[:, g * HEAD_SIZE : (g + 1) * HEAD_SIZE], axis=1, keepdims=True)
                block = jnp.where(lane == g, delta, block)
            turned = jnp.concatenate([block, block], axis=0).T
            norms = norm_t[pl.ds(pl.multiple_of(owner * GROUP, GROUP), GROUP), :]
            st_out[j, :GROUP] = jnp.where(keep, norms, 0.0)
            st_out[j, GROUP:] = jnp.where(keep, turned[:GROUP], 0.0)

            @pl.when(j > 0)
            def _():
                head_copy(ST, j).start()

            @pl.when(j == 0)
            def _():
                own_copy(ST).start()

    gather(0, beside_keys)
    gather_end(0)

    per_step = 6

    def beside_values(j, c):
        if c == 0:

            @pl.when(j == 0)
            def _():
                for i in range(TILES):
                    v_all[i] = v_ring[0, i]

            @pl.when(j == 1)
            def _():
                for part in (Q, DO, ST):
                    head_arrived(part)
                gathered(0)

        @pl.loop(0, per_step // 2)
        def _(i):
            e = (j - 1) * per_step + c * (per_step // 2) + i

            @pl.when((j > 0) & (e < PAIRS))
            def _():
                first_half(e)

    head_arrived(V)
    gather(1, beside_values)
    gather_end(1)

    reduce_start(1)
    gathered(1)

    def beside_dv(j, c):
        @pl.loop(0, 3 - c)
        def _(i):
            second_half(j * 5 + c * 3 + i)

    reduce_ring(1, beside_dv)
    reduce_start(0)
    reduce_end(1)
    head_start(GV)

    def beside_dk(j, c):
        if c == 1:

            @pl.when(j < TILES)
            def _():
                rows = pl.ds(pl.multiple_of(j * TILE, TILE), TILE)
                for g in range(GROUP):
                    part = dq_t[j, :, g * TILE : (g + 1) * TILE] * SCALE
                    dq_out[rows, g * HEAD_SIZE : (g + 1) * HEAD_SIZE] = part.T.astype(BF16)

            @pl.when(j == TILES - 1)
            def _():
                head_start(GQ)

    reduce_ring(0, beside_dk)
    reduce_end(0)
    head_start(GK)

    for w in range(2):

        @pl.loop(0, NZ)
        def _(s, w=w):
            for dy in range(1, NY):
                across_copy(w, s, dy).wait_send()
                cross_back(w, s, dy).wait_send()

        for j in range(HOPS):
            for c in range(2):
                if j < HOPS - 1 or c == 0:
                    up_copy(w, j, c).wait_send()
                if j < HOPS - 1 or c == 1:
                    down_copy(w, j, c).wait_send()
                if j > 0 or c == 0:
                    down_back(w, j, c).wait_send()
                if j > 0 or c == 1:
                    up_back(w, j, c).wait_send()

    for part in (GV, GQ, GK):
        head_arrived(part)
    for part in range(8):
        head_sent(part)


def any_spec():
    return pl.BlockSpec(memory_space=pl.ANY)


def shape(dims, dtype):
    return jax.ShapeDtypeStruct(dims, dtype)


def on_device(queries, outputs, output_gradient, keys, values, log_row_norm, kv_index, counts):
    dma = pltpu.SemaphoreType.DMA
    vmem = pltpu.VMEM
    listed = jnp.arange(ENTRIES, dtype=jnp.int32)[None, :] < counts[:, None]
    lists = jnp.where(listed, kv_index, -1).reshape(NZ * NY, PAIRS)
    padded = jnp.pad(lists, ((0, 0), (0, 128 - PAIRS)), constant_values=-1)

    node = lax.axis_index("ctx")
    tile = lax.dynamic_index_in_dim(lists, node, 0, keepdims=False)
    holder = tile // TILES
    slot = ((node // NY - holder // NY) % NZ) * NY + (node - holder) % NY
    place = jnp.where(holder == node, tile % TILES, TILES + slot)
    place = jnp.where(tile < 0, 0, place)
    number = jnp.arange(PAIRS, dtype=jnp.int32)
    limit = jnp.where(tile == node * TILES + number // ENTRIES, 0, TILE)
    limit = jnp.where(tile < 0, -TILE, limit)
    match = (place.reshape(TILES, 1, ENTRIES) == jnp.arange(PLACES, dtype=jnp.int32)[None, :, None]) & (
        tile >= 0
    ).reshape(TILES, 1, ENTRIES)
    pair = jnp.min(jnp.where(match, number.reshape(TILES, 1, ENTRIES), PAIRS), axis=2).reshape(-1)
    meta = jnp.concatenate([place, limit, pair]).reshape(1, -1)

    block = (TILE, HEAD_SIZE)
    return pl.pallas_call(
        kernel,
        out_shape=(
            shape((ROWS, NH * WIDE), BF16),
            shape((ROWS, NH * HEAD_SIZE), BF16),
            shape((ROWS, NH * HEAD_SIZE), BF16),
        ),
        in_specs=[any_spec()] * 5
        + [pl.BlockSpec(memory_space=pltpu.VMEM)] * 2
        + [pl.BlockSpec(memory_space=pltpu.SMEM)],
        out_specs=(any_spec(),) * 3,
        scratch_shapes=[
            vmem((NZ, TILES) + block, BF16), vmem((NZ, TILES) + block, BF16),
            vmem((PLACES,) + block, BF16), vmem((PLACES,) + block, BF16),
            vmem((2, NZ, NY - 1) + block, BF16),
            vmem((NH * ROWS, WIDE), BF16), vmem((NH * ROWS, WIDE), BF16),
            vmem((ROWS, NH * WIDE), BF16), vmem((ROWS, NH * WIDE), BF16),
            vmem(block, F32), vmem((NH, 2 * GROUP, 128), F32), vmem((NH, 2 * GROUP, 128), F32),
            vmem((NY, NZ, 128), jnp.int32),
            vmem((PAIRS, TILE, GROUP * TILE), F32),
            vmem((PAIRS + 1,) + block, F32), vmem((PAIRS + 1,) + block, F32),
            vmem((TILES, HEAD_SIZE, GROUP * TILE), F32), vmem((NH * ROWS, WIDE), BF16),
            vmem((2, NZ, NY) + block, BF16),
            vmem((NZ, NY - 1) + block, BF16), vmem((NZ, NY - 1) + block, BF16),
            vmem((2, HOPS, TILES) + block, BF16), vmem((2, HOPS, TILES) + block, BF16),
            vmem((HOPS, TILES) + block, BF16), vmem((HOPS, TILES) + block, BF16),
            vmem((HOPS, TILES) + block, BF16), vmem((HOPS, TILES) + block, BF16),
            vmem((TILES,) + block, BF16), vmem((TILES,) + block, BF16),
            dma((8, NH - 1)), dma((8, NH - 1)), dma((8,)), dma((2,)),
            dma((2, HOPS, 2)), dma((2, HOPS, 2)), dma((2, HOPS, 2)), dma((2, HOPS, 2)),
            dma((2, NZ, NY - 1)), dma((2, NZ, NY - 1)),
            dma((2, HOPS, 2)), dma((2, HOPS, 2)), dma((2, HOPS, 2)), dma((2, HOPS, 2)),
            dma((2, NZ, NY - 1)), dma((2, NZ, NY - 1)),
        ],
        compiler_params=pltpu.CompilerParams(collective_id=0, has_side_effects=True, vmem_limit_bytes=63 << 20),
        cost_estimate=pl.CostEstimate(flops=6_710_886_400, bytes_accessed=12 << 20, transcendentals=5_242_880),
        name="attention_backward",
    )(queries, outputs, output_gradient, keys, values, log_row_norm, padded, meta)


def solution(mesh):
    rows = P(("ctx", "head"), None)
    return jax.shard_map(
        on_device,
        mesh=mesh,
        in_specs=(rows,) * 6 + (P(), P()),
        out_specs=(rows,) * 3,
        check_vma=False,
    )
```

time: 1280 us -> 179 us (0.14)
  waiting for transfers between devices: 580 us -> 0 us
  starting transfers between devices: 526 us -> 0 us
  Pallas kernels: 0 us -> 172 us
  local copies, waits for them, and re-layouts: 71.2 us -> 6.39 us
  loops' own time: 33.8 us -> 0 us
  matrix products: 30.3 us -> 0 us
  other arithmetic: 30.4 us -> 0.27 us
    all_to_all x11 -> x0, waiting for transfers between devices: 580 us -> none  [the longest x1 357 us: on_device(): lax.all_to_all(status[1][tiles:tiles + ctx_count], 'ctx', split_axis=0, c...]
    all_to_all x11 -> x0, starting transfers between devices: 526 us -> none  [the longest x1 456 us: on_device(): lax.all_to_all(status[1][tiles:tiles + ctx_count], 'ctx', split_axis=0, c...]
    pallas_call x0 -> x1, Pallas kernels: none -> 172 us  [on_device(): pl.pallas_call(kernel, out_shape=(shape((ROWS, NH * WIDE), BF16), shape((...]
    another operation x4 -> x0, loops' own time: 33.8 us -> none  [on_device(): status = lax.fori_loop(0, counts[query_tile], entry, status)]
    dot_general x37 -> x0, matrix products: 30.3 us -> none  [the longest x7 8.59 us: pairwise_terms(): jnp.einsum('agqk,qagd->kad', score_grad, query_row_block, preferred_eleme...]
    scatter-add x7 -> x0, other arithmetic: 15.3 us -> none  [entry(): pair_sums.at[place].add(pairwise_gradient)]
  transfers between devices with their start and end apart: 11 -> 0, of which waited for: 10 -> 0; matrix products, arithmetic and copies ran while one was open for 4% -> 0% of each run, Pallas kernels for 0% -> 0%
where the time goes in v2:
time: 179 us
  Pallas kernels  172 us (96%)
  local copies, waits for them, and re-layouts  6.39 us (4%)
    pallas_call x1, Pallas kernels, on_device(): pl.pallas_call(kernel, out_shape=(shape((ROWS, NH * WIDE), BF16), shape((...  172 us
    unnamed x11, local copies, waits for them, and re-layouts  4.59 us

profile of v2, /device:TPU:1, one launch (start us, length us, event | category | flops | bytes accessed | tf_op | source)
XLA Modules:
  0.0 179.1 jit_solution(5125830952319729709)
XLA Ops:
  0.6 0.0 copy-start.2
  0.7 0.0 copy-start.3
  0.7 0.7 copy-done.2
  1.4 0.0 copy-done.3
  1.4 0.1 copy.13
  1.5 0.1 reshape.136
  1.6 0.6 pad.4.lists_ref
  2.3 0.1 squeeze.7
  2.4 0.1 copy.15
  2.5 0.1 copy.14
  2.6 0.1 select_reduce_fusion
  2.7 0.1 reshape.140
  2.8 0.1 pad_add_fusion
  2.9 0.6 reshape.141.meta_ref
  3.4 171.8 %attention_backward.1 = (bf16[64,8192]{1,0:T(8,128)(2,1)}, bf16[64,1024]{1,0:T(8,128)(2,1)}, bf16[64,1024]{1,0:T(8,128)(2,1)}) custom-call(bf16[64,8192]{1,0:T(8,128)(2,1)} %q_ref.1, bf16[64,8192]{1,0:T(8,128)(2,1)} %o_ref.1, bf16[64,8192]{1,0:T(8,128)(2,1)} %do_ref.1, bf16[64,1024]{1,0:T(8,128)(2,1)} %k_ref.1, bf16[64,1024]{1,0:T(8,128)(2,1)} %v_ref.1, ...), custom_call_target="tpu_custom_call" | custom-call | flops 6710886400 | bytes 12582912 | tf_op jit(solution)/shard_map/attention_backward/pallas_call | solution.py:550
  175.2 0.0 copy-start.1
  175.2 2.3 %copy.19 = bf16[64,8192]{1,0:T(8,128)(2,1)} copy(bf16[64,8192]{1,0:T(8,128)(2,1)} %get-tuple-element.8) | data formatting | bytes 2097152
  177.5 0.0 copy-done.1
  177.5 0.0 copy-start
  177.5 0.7 copy.20
  178.2 0.3 copy-done
  178.5 0.7 copy.21
  (6 shorter events, 0.1 us)
Async XLA Ops:
  0.6 0.7 copy-start.2
  0.7 0.7 copy-start.3
  175.2 2.3 %copy-start.1 = (bf16[64,1024]{1,0:T(8,128)(2,1)S(1)}, bf16[64,1024]{1,0:T(8,128)(2,1)}, u32[]{:S(2)}) copy-start(bf16[64,1024]{1,0:T(8,128)(2,1)} %get-tuple-element.9) | copy-start | bytes 393220
  177.5 1.0 copy-start

commit v3 on v2

v3 whole, which is shorter than its diff:
```python
import math

import jax
import jax.numpy as jnp
from jax import lax
from jax.experimental import pallas as pl
from jax.experimental.pallas import tpu as pltpu
from jax.sharding import PartitionSpec as P

QUERY_HEADS = 64
KEY_VALUE_HEADS = 8
HEAD_SIZE = 128
TILE = 128
GROUP = QUERY_HEADS // KEY_VALUE_HEADS
TILES = 4
ENTRIES = 10
PAIRS = TILES * ENTRIES
NZ = 16
NY = 4
NH = 8
HOPS = NZ // 2
PLACES = TILES + (HOPS + 1) * NY * 2
LAG = 2
BACK_LAG = 3
PER_HOP = -(-PAIRS // 2 // BACK_LAG)
CHUNK = TILES // 2
ROWS = 64
WIDE = GROUP * HEAD_SIZE
SCALE = HEAD_SIZE ** (-0.5)
LOG2E = math.log2(math.e)
MESH = pl.DeviceIdType.MESH
F32 = jnp.float32
BF16 = jnp.bfloat16
NT = (((1,), (1,)), ((), ()))
TN = (((0,), (0,)), ((), ()))

K, V, Q, DO, ST, GQ, GV, GK = range(8)


def kernel(
    q_ref, o_ref, do_ref, k_ref, v_ref, norm_ref, lists_ref, meta_ref,
    gq_ref, gk_ref, gv_ref,
    k_ring, v_ring, k_all, v_all, picked, q_all, do_all, o_own, do_own, norm_t, st_out, st_all, sel,
    weights, dv_pairs, dk_pairs, dq_t, dq_out, terms, dv_across, dk_across, down_out, up_out,
    dv_down, dv_up, dk_down, dk_up, dv_done, dk_done,
    x_send, x_recv, local, own_sem,
    u_send, u_recv, d_send, d_recv, y_send, y_recv,
    bu_send, bu_recv, bd_send, bd_recv, by_send, by_recv,
):
    ctx = lax.axis_index("ctx")
    h, z, y = lax.axis_index("head"), ctx // NY, lax.rem(ctx, NY)
    above = lax.rem(z + 1, NZ) * NY + y
    below = lax.rem(z + NZ - 1, NZ) * NY + y

    barrier = pltpu.get_barrier_semaphore()

    def greet(**where):
        pl.semaphore_signal(barrier, inc=1, device_id=where, device_id_type=MESH)

    for d in range(1, NH):
        greet(head=lax.rem(h + d, NH))
    for d in range(1, NY):
        greet(ctx=z * NY + lax.rem(y + d, NY))
    greet(ctx=above)
    greet(ctx=below)

    own_load = [
        pltpu.make_async_copy(o_ref, o_own, own_sem.at[0]),
        pltpu.make_async_copy(do_ref, do_own, own_sem.at[1]),
    ]
    for copy in own_load:
        copy.start()
    pl.semaphore_wait(barrier, NH + NY)

    def columns(owner, width):
        return pl.ds(pl.multiple_of(owner * width, width), width)

    def half(owner):
        return pl.ds(pl.multiple_of(lax.rem(owner, 2) * ROWS, ROWS), ROWS)

    def rows_of(owner):
        return pl.ds(pl.multiple_of(owner * ROWS, ROWS), ROWS)

    def head_ends(part, owner, d):
        if part == K:
            return k_ref.at[:, columns(owner, HEAD_SIZE)], k_ring.at[0, h // 2, half(h), :]
        if part == V:
            return v_ref.at[:, columns(owner, HEAD_SIZE)], v_ring.at[0, h // 2, half(h), :]
        if part == Q:
            return q_ref.at[:, columns(owner, WIDE)], q_all.at[rows_of(h), :]
        if part == DO:
            return do_ref.at[:, columns(owner, WIDE)], do_all.at[rows_of(h), :]
        if part == ST:
            return st_out.at[d], st_all.at[h]
        if part == GQ:
            return dq_out.at[rows_of(owner), :], gq_ref.at[:, columns(h, WIDE)]
        if part == GV:
            return dv_done.at[owner // 2, half(owner), :], gv_ref.at[:, columns(h, HEAD_SIZE)]
        return dk_done.at[owner // 2, half(owner), :], gk_ref.at[:, columns(h, HEAD_SIZE)]

    def head_copy(part, d):
        owner = lax.rem(h + d, NH)
        src, dst = head_ends(part, owner, d)
        return pltpu.make_async_remote_copy(
            src_ref=src, dst_ref=dst, send_sem=x_send.at[part, d - 1], recv_sem=x_recv.at[part, d - 1],
            device_id={"head": owner}, device_id_type=MESH,
        )

    def own_copy(part):
        src, dst = head_ends(part, h, 0)
        return pltpu.make_async_copy(src, dst, local.at[part])

    def head_start(part):
        for d in range(1, NH):
            head_copy(part, d).start()
        own_copy(part).start()

    def head_arrived(part):
        own_copy(part).wait()
        for d in range(1, NH):
            head_copy(part, d).wait_recv()

    def head_sent(part):
        for d in range(1, NH):
            head_copy(part, d).wait_send()

    ring_of, all_of = (k_ring, v_ring), (k_all, v_all)

    def tiles(c):
        return pl.ds(c * CHUNK, CHUNK)

    def up_copy(w, j, c):
        ring = ring_of[w]
        return pltpu.make_async_remote_copy(
            src_ref=ring.at[j, tiles(c)], dst_ref=ring.at[j + 1, tiles(c)],
            send_sem=u_send.at[w, j, c], recv_sem=u_recv.at[w, j, c],
            device_id={"ctx": above}, device_id_type=MESH,
        )

    def down_copy(w, j, c):
        ring = ring_of[w]
        return pltpu.make_async_remote_copy(
            src_ref=ring.at[lax.rem(NZ - j, NZ), tiles(c)], dst_ref=ring.at[NZ - 1 - j, tiles(c)],
            send_sem=d_send.at[w, j, c], recv_sem=d_recv.at[w, j, c],
            device_id={"ctx": below}, device_id_type=MESH,
        )

    def across_copy(w, j, dy, sides):
        return pltpu.make_async_remote_copy(
            src_ref=picked.at[w, j, dy - 1, pl.ds(0, sides)],
            dst_ref=all_of[w].at[pl.ds(TILES + (j * NY + dy) * 2, sides)],
            send_sem=y_send.at[w, j, dy - 1], recv_sem=y_recv.at[w, j, dy - 1],
            device_id={"ctx": z * NY + lax.rem(y + dy, NY)}, device_id_type=MESH,
        )

    def pick(w, s, j, side):
        ring = ring_of[w]
        for dy in range(NY):
            want = sel[dy, pl.ds(s, 1), :]
            for c in range(TILES):
                term = ring[s, c] * (want == c).astype(F32).astype(BF16)
                total = term if c == 0 else total + term
            if dy == 0:
                all_of[w][TILES + j * NY * 2 + side] = total
            else:
                picked[w, j, dy - 1, side] = total

    def picks(w, j):
        pick(w, j, j, 0)

        @pl.when(j > 0)
        def _():
            pick(w, NZ - j, j, 1)
            for dy in range(1, NY):
                across_copy(w, j, dy, 2).start()

        @pl.when(j == 0)
        def _():
            for dy in range(1, NY):
                across_copy(w, j, dy, 1).start()

    def serve(w, j, c):
        @pl.when(j > 0)
        def _():
            up_copy(w, j - 1, c).wait_recv()

        @pl.when((j < HOPS - 1) | (c == 0))
        def _():
            up_copy(w, j, c).start()

        @pl.when(j > 0)
        def _():
            down_copy(w, j - 1, c).wait_recv()

        @pl.when((j < HOPS - 1) | (c == 1))
        def _():
            down_copy(w, j, c).start()

    def gather_end(w):
        up_copy(w, HOPS - 1, 0).wait_recv()
        down_copy(w, HOPS - 1, 1).wait_recv()
        pick(w, HOPS, HOPS, 0)
        for dy in range(1, NY):
            across_copy(w, HOPS, dy, 1).start()

    def gathered(w):
        @pl.loop(1, HOPS)
        def _(j):
            for dy in range(1, NY):
                across_copy(w, j, dy, 2).wait_recv()

        for j in (0, HOPS):
            for dy in range(1, NY):
                across_copy(w, j, dy, 1).wait_recv()

    order = lax.broadcasted_iota(jnp.int32, (TILE, GROUP * TILE), 0) - lax.rem(
        lax.broadcasted_iota(jnp.int32, (TILE, GROUP * TILE), 1), TILE
    )

    def all_heads(ref, t):
        rows = pl.ds(pl.multiple_of(t * TILE, TILE), TILE)
        return jnp.concatenate([ref[rows, g * HEAD_SIZE : (g + 1) * HEAD_SIZE] for g in range(GROUP)], axis=0)

    def stat_rows(t, first):
        both = st_all[2 * t] + st_all[2 * t + 1]
        return jnp.concatenate([both[first + g : first + g + 1] for g in range(GROUP)], axis=1)

    def two_tiles(ref, e):
        return jnp.concatenate([ref[meta_ref[0, e]], ref[meta_ref[0, e + 1]]], axis=0)

    def first_half(b):
        e = 2 * b
        t = e // ENTRIES
        scores = lax.dot_general(two_tiles(k_all, e), all_heads(q_all, t), NT, preferred_element_type=F32)
        full = jnp.exp2(scores * (SCALE * LOG2E) - stat_rows(t, 0))
        parts = []
        for i in range(2):
            part = jnp.where(order <= meta_ref[0, PAIRS + e + i], full[i * TILE : (i + 1) * TILE], 0.0)
            weights[e + i] = part
            parts.append(part.astype(BF16))
        dv = jnp.dot(jnp.concatenate(parts, axis=0), all_heads(do_all, t), preferred_element_type=F32)
        for i in range(2):
            dv_pairs[e + i] = dv[i * TILE : (i + 1) * TILE]

    def second_half(b):
        e = 2 * b
        t = e // ENTRIES
        dp = lax.dot_general(two_tiles(v_all, e), all_heads(do_all, t), NT, preferred_element_type=F32)
        delta = stat_rows(t, GROUP)
        parts = [(weights[e + i] * (dp[i * TILE : (i + 1) * TILE] - delta)).astype(BF16) for i in range(2)]
        score_grad = jnp.concatenate(parts, axis=0)
        dk = jnp.dot(score_grad, all_heads(q_all, t), preferred_element_type=F32) * SCALE
        for i in range(2):
            dk_pairs[e + i] = dk[i * TILE : (i + 1) * TILE]
        dq_t[t] += lax.dot_general(two_tiles(k_all, e), score_grad, TN, preferred_element_type=F32)

    pairs_of, cross_of, done_of = (dk_pairs, dv_pairs), (dk_across, dv_across), (dk_done, dv_done)
    down_of, up_of = (dk_down, dv_down), (dk_up, dv_up)

    def cross_back(w, j, dy, sides):
        return pltpu.make_async_remote_copy(
            src_ref=terms.at[w, j, dy, pl.ds(0, sides)], dst_ref=cross_of[w].at[j, dy - 1, pl.ds(0, sides)],
            send_sem=by_send.at[w, j, dy - 1], recv_sem=by_recv.at[w, j, dy - 1],
            device_id={"ctx": z * NY + lax.rem(y + NY - dy, NY)}, device_id_type=MESH,
        )

    def down_back(w, j, c):
        return pltpu.make_async_remote_copy(
            src_ref=down_out.at[w, j, tiles(c)], dst_ref=down_of[w].at[j, tiles(c)],
            send_sem=bd_send.at[w, j, c], recv_sem=bd_recv.at[w, j, c],
            device_id={"ctx": below}, device_id_type=MESH,
        )

    def up_back(w, j, c):
        return pltpu.make_async_remote_copy(
            src_ref=up_out.at[w, j, tiles(c)], dst_ref=up_of[w].at[j, tiles(c)],
            send_sem=bu_send.at[w, j, c], recv_sem=bu_recv.at[w, j, c],
            device_id={"ctx": above}, device_id_type=MESH,
        )

    def place_sum(w, place):
        for t in range(TILES):
            term = pairs_of[w][meta_ref[0, 2 * PAIRS + t * PLACES + place]]
            total = term if t == 0 else total + term
        return total

    def give(w, j, sides):
        for dy in range(NY):
            for side in range(sides):
                terms[w, j, dy, side] = place_sum(w, TILES + (j * NY + dy) * 2 + side).astype(BF16)
            if dy > 0:
                cross_back(w, j, dy, sides).start()

    def taken(w, j, sides):
        for dy in range(1, NY):
            cross_back(w, j, dy, sides).wait_recv()

    def asked(w, s, j, side, c, first):
        total = None
        for dy in range(first, NY):
            weight = (sel[dy, pl.ds(s, 1), :] == c).astype(F32)
            block = terms[w, j, 0, side] if dy == 0 else cross_of[w][j, dy - 1, side]
            term = block.astype(F32) * weight
            total = term if total is None else total + term
        return total

    def reduce_start(w):
        give(w, HOPS, 1)
        for j in (HOPS - 1, HOPS - 2):
            give(w, j, 2)
        for c in range(CHUNK):
            down_of[w][0, CHUNK + c] = jnp.zeros((TILE, HEAD_SIZE), BF16)
            up_of[w][0, c] = jnp.zeros((TILE, HEAD_SIZE), BF16)

    def hop(w, j, c, out, into, side, copy, first):
        slot = HOPS + j if side == 1 else HOPS - j

        if c == first:

            @pl.when(j == 0)
            def _():
                for i in range(c * CHUNK, (c + 1) * CHUNK):
                    out[w, 0, i] = asked(w, HOPS, HOPS, 0, i, 0).astype(BF16)
                copy(w, j, c).start()

            @pl.when(j > 0)
            def _():
                copy(w, j - 1, c).wait_recv()

        else:

            @pl.when(j > 1)
            def _():
                copy(w, j - 1, c).wait_recv()

        @pl.when(j > 0)
        def _():
            for i in range(c * CHUNK, (c + 1) * CHUNK):
                part = asked(w, slot, HOPS - j, side, i, 0)
                out[w, j, i] = (part + into[j - 1, i].astype(F32)).astype(BF16)
            copy(w, j, c).start()

    def take(w, j):
        @pl.when(j == 0)
        def _():
            taken(w, HOPS - j, 1)

        @pl.when(j > 0)
        def _():
            taken(w, HOPS - j, 2)

    def hops(w, j, c):
        hop(w, j, c, down_out, down_of[w], 0, down_back, 0)
        hop(w, j, c, up_out, up_of[w], 1, up_back, 1)

    def give_next(w, j):
        @pl.when(j < HOPS - 3)
        def _():
            give(w, HOPS - 3 - j, 2)

        @pl.when(j == HOPS - 3)
        def _():
            give(w, HOPS - 3 - j, 1)

    def reduce_end(w):
        taken(w, 0, 1)
        for i in range(TILES):
            c = i // CHUNK
            part = place_sum(w, i) + asked(w, 0, 0, 0, i, 1)
            if i % CHUNK == 0:
                down_back(w, HOPS - 1, c).wait_recv()
                up_back(w, HOPS - 1, c).wait_recv()
            part += down_of[w][HOPS - 1, i].astype(F32)
            part += up_of[w][HOPS - 1, i].astype(F32)
            done_of[w][i] = part.astype(BF16)

    head_start(K)
    slot = lax.broadcasted_iota(jnp.int32, (NZ, 128), 0)
    plane = lax.rem(z - slot + NZ, NZ)
    for dy in range(NY):
        node = z * NY + lax.rem(y + dy, NY)
        entries = lists_ref[pl.ds(node, 1), :]
        match = (entries >> 2) == plane * NY + y
        found = jnp.max(jnp.where(match, entries & 3, -1), axis=1, keepdims=True)
        sel[dy] = jnp.broadcast_to(found, (NZ, 128))
    head_arrived(K)

    lane = lax.broadcasted_iota(jnp.int32, (ROWS, 128), 1)
    keep = (lax.broadcasted_iota(jnp.int32, (GROUP, 128), 1) >= ROWS) == (lax.rem(h, 2) == 1)

    def prepare(i):
        @pl.when(i == 0)
        def _():
            for copy in own_load:
                copy.wait()
            block = jnp.concatenate([norm_ref[...], jnp.zeros((ROWS, ROWS), F32)], axis=1) * LOG2E
            norm_t[...] = jnp.concatenate([block, block], axis=0).T
            for t in range(TILES):
                k_all[t] = k_ring[0, t]
                dq_t[t] = jnp.zeros((HEAD_SIZE, GROUP * TILE), F32)
            dv_pairs[PAIRS] = jnp.zeros((TILE, HEAD_SIZE), F32)
            dk_pairs[PAIRS] = jnp.zeros((TILE, HEAD_SIZE), F32)

        owner = lax.rem(h + i, NH)
        cols = columns(owner, WIDE)
        product = do_own[:, cols].astype(F32) * o_own[:, cols].astype(F32)
        block = jnp.zeros((ROWS, 128), F32)
        for g in range(GROUP):
            delta = jnp.sum(product[:, g * HEAD_SIZE : (g + 1) * HEAD_SIZE], axis=1, keepdims=True)
            block = jnp.where(lane == g, delta, block)
        turned = jnp.concatenate([block, block], axis=0).T
        norms = norm_t[pl.ds(pl.multiple_of(owner * GROUP, GROUP), GROUP), :]
        st_out[i, :GROUP] = jnp.where(keep, norms, 0.0)
        st_out[i, GROUP:] = jnp.where(keep, turned[:GROUP], 0.0)

        @pl.when(i > 0)
        def _():
            head_copy(ST, i).start()

        @pl.when(i == 0)
        def _():
            own_copy(ST).start()

    @pl.loop(0, HOPS)
    def _(i):
        @pl.when(i == LAG)
        def _():
            head_arrived(V)
            for t in range(TILES):
                v_all[t] = v_ring[0, t]

        for c in range(2):
            serve(0, i, c)

            @pl.when(i >= LAG)
            def _():
                serve(1, i - LAG, c)

            if c == 0:

                @pl.when(i == 0)
                def _():
                    head_start(V)

        @pl.when(i == 0)
        def _():
            head_start(Q)
            head_start(DO)

        picks(0, i)

        @pl.when(i >= LAG)
        def _():
            picks(1, i - LAG)

        prepare(i)

    gather_end(0)

    @pl.loop(HOPS, HOPS + LAG - 1)
    def _(i):
        for c in range(2):
            serve(1, i - LAG, c)
        picks(1, i - LAG)

    for part in (Q, DO, ST):
        head_arrived(part)
    gathered(0)

    @pl.loop(0, PAIRS // 2)
    def _(b):
        first_half(b)

        @pl.when(b == 3)
        def _():
            serve(1, b - 3 + HOPS - 1, 0)

        @pl.when(b == 5)
        def _():
            serve(1, b - 5 + HOPS - 1, 1)
            picks(1, b - 5 + HOPS - 1)

        @pl.when(b == 11)
        def _():
            gather_end(1)

    reduce_start(1)
    gathered(1)

    @pl.loop(0, HOPS + BACK_LAG)
    def _(i):
        first, second = i < HOPS, i >= BACK_LAG
        j = i - BACK_LAG

        @pl.when(i == BACK_LAG)
        def _():
            reduce_start(0)

        @pl.when(i == HOPS)
        def _():
            reduce_end(1)
            head_start(GV)

        @pl.when(first)
        def _():
            take(1, i)

        for c in range(2):

            @pl.when(first)
            def _():
                hops(1, i, c)
                if c == 1:
                    give_next(1, i)

            if c == 0:

                @pl.when(second)
                def _():
                    take(0, j)

            @pl.when(second)
            def _():
                hops(0, j, c)
                if c == 1:
                    give_next(0, j)

            @pl.when(i < BACK_LAG)
            def _():
                @pl.loop(0, (PER_HOP + 1 - c) // 2)
                def _(n):
                    b = i * PER_HOP + c * ((PER_HOP + 1) // 2) + n

                    @pl.when(b < PAIRS // 2)
                    def _():
                        second_half(b)

        @pl.when(second & (j < TILES))
        def _():
            rows = pl.ds(pl.multiple_of(j * TILE, TILE), TILE)
            for g in range(GROUP):
                part = dq_t[j, :, g * TILE : (g + 1) * TILE] * SCALE
                dq_out[rows, g * HEAD_SIZE : (g + 1) * HEAD_SIZE] = part.T.astype(BF16)

        @pl.when(j == TILES - 1)
        def _():
            head_start(GQ)

    reduce_end(0)
    head_start(GK)

    for w in range(2):

        @pl.loop(1, HOPS)
        def _(j, w=w):
            for dy in range(1, NY):
                across_copy(w, j, dy, 2).wait_send()
                cross_back(w, j, dy, 2).wait_send()

        for j in (0, HOPS):
            for dy in range(1, NY):
                across_copy(w, j, dy, 1).wait_send()
                cross_back(w, j, dy, 1).wait_send()

        for j in range(HOPS):
            for c in range(2):
                if j < HOPS - 1 or c == 0:
                    up_copy(w, j, c).wait_send()
                if j < HOPS - 1 or c == 1:
                    down_copy(w, j, c).wait_send()
                if j > 0 or c == 0:
                    down_back(w, j, c).wait_send()
                if j > 0 or c == 1:
                    up_back(w, j, c).wait_send()

    for part in (GV, GQ, GK):
        head_arrived(part)
    for part in range(8):
        head_sent(part)


PIECES = 4


def hand_over(gq_ref, gk_ref, gv_ref, gq_out, gk_out, gv_out):
    gq_out[...] = gq_ref[...]
    gk_out[...] = gk_ref[...]
    gv_out[...] = gv_ref[...]


def any_spec():
    return pl.BlockSpec(memory_space=pl.ANY)


def shape(dims, dtype):
    return jax.ShapeDtypeStruct(dims, dtype)


def on_device(queries, outputs, output_gradient, keys, values, log_row_norm, kv_index, counts):
    dma = pltpu.SemaphoreType.DMA
    vmem = pltpu.VMEM
    listed = jnp.arange(ENTRIES, dtype=jnp.int32)[None, :] < counts[:, None]
    lists = jnp.where(listed, kv_index, -1).reshape(NZ * NY, PAIRS)
    padded = jnp.pad(lists, ((0, 0), (0, 128 - PAIRS)), constant_values=-1)

    node = lax.axis_index("ctx")
    tile = lax.dynamic_index_in_dim(lists, node, 0, keepdims=False)
    holder = tile // TILES
    away = (node // NY - holder // NY) % NZ
    slot = (jnp.minimum(away, NZ - away) * NY + (node - holder) % NY) * 2 + (away > HOPS)
    place = jnp.where(holder == node, tile % TILES, TILES + slot)
    place = jnp.where(tile < 0, 0, place)
    number = jnp.arange(PAIRS, dtype=jnp.int32)
    limit = jnp.where(tile == node * TILES + number // ENTRIES, 0, TILE)
    limit = jnp.where(tile < 0, -TILE, limit)
    match = (place.reshape(TILES, 1, ENTRIES) == jnp.arange(PLACES, dtype=jnp.int32)[None, :, None]) & (
        tile >= 0
    ).reshape(TILES, 1, ENTRIES)
    pair = jnp.min(jnp.where(match, number.reshape(TILES, 1, ENTRIES), PAIRS), axis=2).reshape(-1)
    meta = jnp.concatenate([place, limit, pair]).reshape(1, -1)

    block = (TILE, HEAD_SIZE)
    grads = pl.pallas_call(
        kernel,
        out_shape=(
            shape((ROWS, NH * WIDE), BF16),
            shape((ROWS, NH * HEAD_SIZE), BF16),
            shape((ROWS, NH * HEAD_SIZE), BF16),
        ),
        in_specs=[any_spec()] * 5
        + [pl.BlockSpec(memory_space=pltpu.VMEM)] * 2
        + [pl.BlockSpec(memory_space=pltpu.SMEM)],
        out_specs=(any_spec(),) * 3,
        scratch_shapes=[
            vmem((NZ, TILES) + block, BF16), vmem((NZ, TILES) + block, BF16),
            vmem((PLACES,) + block, BF16), vmem((PLACES,) + block, BF16),
            vmem((2, HOPS + 1, NY - 1, 2) + block, BF16),
            vmem((NH * ROWS, WIDE), BF16), vmem((NH * ROWS, WIDE), BF16),
            vmem((ROWS, NH * WIDE), BF16), vmem((ROWS, NH * WIDE), BF16),
            vmem(block, F32), vmem((NH, 2 * GROUP, 128), F32), vmem((NH, 2 * GROUP, 128), F32),
            vmem((NY, NZ, 128), jnp.int32),
            vmem((PAIRS, TILE, GROUP * TILE), F32),
            vmem((PAIRS + 1,) + block, F32), vmem((PAIRS + 1,) + block, F32),
            vmem((TILES, HEAD_SIZE, GROUP * TILE), F32), vmem((NH * ROWS, WIDE), BF16),
            vmem((2, HOPS + 1, NY, 2) + block, BF16),
            vmem((HOPS + 1, NY - 1, 2) + block, BF16), vmem((HOPS + 1, NY - 1, 2) + block, BF16),
            vmem((2, HOPS, TILES) + block, BF16), vmem((2, HOPS, TILES) + block, BF16),
            vmem((HOPS, TILES) + block, BF16), vmem((HOPS, TILES) + block, BF16),
            vmem((HOPS, TILES) + block, BF16), vmem((HOPS, TILES) + block, BF16),
            vmem((TILES,) + block, BF16), vmem((TILES,) + block, BF16),
            dma((8, NH - 1)), dma((8, NH - 1)), dma((8,)), dma((2,)),
            dma((2, HOPS, 2)), dma((2, HOPS, 2)), dma((2, HOPS, 2)), dma((2, HOPS, 2)),
            dma((2, HOPS + 1, NY - 1)), dma((2, HOPS + 1, NY - 1)),
            dma((2, HOPS, 2)), dma((2, HOPS, 2)), dma((2, HOPS, 2)), dma((2, HOPS, 2)),
            dma((2, HOPS + 1, NY - 1)), dma((2, HOPS + 1, NY - 1)),
        ],
        compiler_params=pltpu.CompilerParams(collective_id=0, has_side_effects=True, vmem_limit_bytes=63 << 20),
        cost_estimate=pl.CostEstimate(flops=6_710_886_400, bytes_accessed=12 << 20, transcendentals=5_242_880),
        name="attention_backward",
    )(queries, outputs, output_gradient, keys, values, log_row_norm, padded, meta)
    return pl.pallas_call(
        hand_over,
        out_shape=tuple(shape(grad.shape, grad.dtype) for grad in grads),
        grid=(PIECES,),
        in_specs=[pl.BlockSpec((ROWS // PIECES, grad.shape[1]), lambda i: (i, 0)) for grad in grads],
        out_specs=tuple(pl.BlockSpec((ROWS // PIECES, grad.shape[1]), lambda i: (i, 0)) for grad in grads),
        name="hand_over",
    )(*grads)


def solution(mesh):
    rows = P(("ctx", "head"), None)
    return jax.shard_map(
        on_device,
        mesh=mesh,
        in_specs=(rows,) * 6 + (P(), P()),
        out_specs=(rows,) * 3,
        check_vma=False,
    )
```

time: 179 us -> 156 us (0.87)
  Pallas kernels: 172 us -> 152 us
  local copies, waits for them, and re-layouts: 6.39 us -> 2.48 us
    pallas_call x1, Pallas kernels: 172 us -> 149 us  [on_device(): pl.pallas_call(kernel, out_shape=(shape((ROWS, NH * WIDE), BF16), shape((...]
    unnamed x11 -> x4, local copies, waits for them, and re-layouts: 4.59 us -> 0.68 us
    pallas_call x0 -> x1, Pallas kernels: none -> 3.46 us  [on_device(): pl.pallas_call(hand_over, out_shape=tuple((shape(grad.shape, grad.dtype)...]
where the time goes in v3:
time: 156 us
  Pallas kernels  152 us (97%)
  local copies, waits for them, and re-layouts  2.48 us (2%)
    pallas_call x1, Pallas kernels, on_device(): pl.pallas_call(kernel, out_shape=(shape((ROWS, NH * WIDE), BF16), shape((...  149 us
    pallas_call x1, Pallas kernels, on_device(): pl.pallas_call(hand_over, out_shape=tuple((shape(grad.shape, grad.dtype)...  3.46 us

profile of v3, /device:TPU:1, one launch (start us, length us, event | category | flops | bytes accessed | tf_op | source)
XLA Modules:
  0.0 155.7 jit_solution(144766385664631303)
XLA Ops:
  0.6 0.0 copy-start
  0.7 0.0 copy-start.1
  0.7 0.7 copy-done
  1.4 0.0 copy-done.1
  1.4 0.1 copy.13
  1.5 0.1 reshape.142
  1.6 0.6 pad.4.lists_ref
  2.3 0.1 squeeze.7
  2.4 0.1 copy.15
  2.5 0.1 copy.14
  2.6 0.1 select_reduce_fusion
  2.7 0.1 reshape.146
  2.8 0.1 pad_add_fusion
  2.9 0.6 reshape.147.meta_ref
  3.4 148.8 %attention_backward.1 = (bf16[64,8192]{1,0:T(8,128)(2,1)}, bf16[64,1024]{1,0:T(8,128)(2,1)}, bf16[64,1024]{1,0:T(8,128)(2,1)}) custom-call(bf16[64,8192]{1,0:T(8,128)(2,1)} %q_ref.1, bf16[64,8192]{1,0:T(8,128)(2,1)} %o_ref.1, bf16[64,8192]{1,0:T(8,128)(2,1)} %do_ref.1, bf16[64,1024]{1,0:T(8,128)(2,1)} %k_ref.1, bf16[64,1024]{1,0:T(8,128)(2,1)} %v_ref.1, ...), custom_call_target="tpu_custom_call" | custom-call | flops 6710886400 | bytes 12582912 | tf_op jit(solution)/shard_map/attention_backward/pallas_call | solution.py:623
  152.3 3.5 %hand_over.1 = (bf16[64,8192]{1,0:T(8,128)(2,1)}, bf16[64,1024]{1,0:T(8,128)(2,1)}, bf16[64,1024]{1,0:T(8,128)(2,1)}) custom-call(bf16[64,8192]{1,0:T(8,128)(2,1)} %get-tuple-element.6.gq_ref, bf16[64,1024]{1,0:T(8,128)(2,1)} %get-tuple-element.7.gk_ref, bf16[64,1024]{1,0:T(8,128)(2,1)} %get-tuple-element.8.gv_ref), custom_call_target="tpu_custom_call" | custom-call | tf_op jit(solution)/shard_map/hand_over/pallas_call | solution.py:661
  (6 shorter events, 0.1 us)
Async XLA Ops:
  0.6 0.7 copy-start
  0.7 0.7 copy-start.1

commit v4 on v3

--- a/solution.py
+++ b/solution.py
@@ -21,7 +21,7 @@
 HOPS = NZ // 2
 PLACES = TILES + (HOPS + 1) * NY * 2
 LAG = 2
-BACK_LAG = 3
+BACK_LAG = 2
 PER_HOP = -(-PAIRS // 2 // BACK_LAG)
 CHUNK = TILES // 2
 ROWS = 64
@@ -252,7 +252,12 @@
         dk = jnp.dot(score_grad, all_heads(q_all, t), preferred_element_type=F32) * SCALE
         for i in range(2):
             dk_pairs[e + i] = dk[i * TILE : (i + 1) * TILE]
-        dq_t[t] += lax.dot_general(two_tiles(k_all, e), score_grad, TN, preferred_element_type=F32)
+            weights[e + i] = parts[i].astype(F32)
+
+    def query_part(b):
+        e = 2 * b
+        score_grad = jnp.concatenate([weights[e], weights[e + 1]], axis=0).astype(BF16)
+        dq_t[e // ENTRIES] += lax.dot_general(two_tiles(k_all, e), score_grad, TN, preferred_element_type=F32)
 
     pairs_of, cross_of, done_of = (dk_pairs, dv_pairs), (dk_across, dv_across), (dk_done, dv_done)
     down_of, up_of = (dk_down, dv_down), (dk_up, dv_up)
@@ -442,17 +447,16 @@
                 def _():
                     head_start(V)
 
+                @pl.when(i > LAG)
+                def _():
+                    picks(1, i - 1 - LAG)
+
         @pl.when(i == 0)
         def _():
             head_start(Q)
             head_start(DO)
 
         picks(0, i)
-
-        @pl.when(i >= LAG)
-        def _():
-            picks(1, i - LAG)
-
         prepare(i)
 
     gather_end(0)
@@ -461,7 +465,8 @@
     def _(i):
         for c in range(2):
             serve(1, i - LAG, c)
-        picks(1, i - LAG)
+            if c == 0:
+                picks(1, i - 1 - LAG)
 
     for part in (Q, DO, ST):
         head_arrived(part)
@@ -474,6 +479,7 @@
         @pl.when(b == 3)
         def _():
             serve(1, b - 3 + HOPS - 1, 0)
+            picks(1, b - 3 + HOPS - 2)
 
         @pl.when(b == 5)
         def _():
@@ -510,7 +516,7 @@
             @pl.when(first)
             def _():
                 hops(1, i, c)
-                if c == 1:
+                if c == 0:
                     give_next(1, i)
 
             if c == 0:
@@ -537,6 +543,10 @@
 
         @pl.when(second & (j < TILES))
         def _():
+            @pl.loop(0, ENTRIES // 2)
+            def _(n):
+                query_part(j * (ENTRIES // 2) + n)
+
             rows = pl.ds(pl.multiple_of(j * TILE, TILE), TILE)
             for g in range(GROUP):
                 part = dq_t[j, :, g * TILE : (g + 1) * TILE] * SCALE

time: 156 us -> 153 us (0.981)
  Pallas kernels: 152 us -> 150 us
    pallas_call x1, Pallas kernels: 149 us -> 146 us  [on_device(): pl.pallas_call(kernel, out_shape=(shape((ROWS, NH * WIDE), BF16), shape((...]
where the time goes in v4:
time: 153 us
  Pallas kernels  150 us (98%)
  local copies, waits for them, and re-layouts  2.48 us (2%)
    pallas_call x1, Pallas kernels, on_device(): pl.pallas_call(kernel, out_shape=(shape((ROWS, NH * WIDE), BF16), shape((...  146 us
    pallas_call x1, Pallas kernels, on_device(): pl.pallas_call(hand_over, out_shape=tuple((shape(grad.shape, grad.dtype)...  3.46 us

profile of v4, /device:TPU:1, one launch (start us, length us, event | category | flops | bytes accessed | tf_op | source)
XLA Modules:
  0.0 153.1 jit_solution(14852139987564120513)
XLA Ops:
  0.6 0.0 copy-start
  0.7 0.0 copy-start.1
  0.7 0.7 copy-done
  1.4 0.0 copy-done.1
  1.4 0.1 copy.13
  1.5 0.1 reshape.142
  1.6 0.6 pad.4.lists_ref
  2.3 0.1 squeeze.7
  2.4 0.1 copy.15
  2.5 0.1 copy.14
  2.6 0.1 select_reduce_fusion
  2.7 0.1 reshape.146
  2.8 0.1 pad_add_fusion
  2.9 0.6 reshape.147.meta_ref
  3.4 146.2 %attention_backward.1 = (bf16[64,8192]{1,0:T(8,128)(2,1)}, bf16[64,1024]{1,0:T(8,128)(2,1)}, bf16[64,1024]{1,0:T(8,128)(2,1)}) custom-call(bf16[64,8192]{1,0:T(8,128)(2,1)} %q_ref.1, bf16[64,8192]{1,0:T(8,128)(2,1)} %o_ref.1, bf16[64,8192]{1,0:T(8,128)(2,1)} %do_ref.1, bf16[64,1024]{1,0:T(8,128)(2,1)} %k_ref.1, bf16[64,1024]{1,0:T(8,128)(2,1)} %v_ref.1, ...), custom_call_target="tpu_custom_call" | custom-call | flops 6710886400 | bytes 12582912 | tf_op jit(solution)/shard_map/attention_backward/pallas_call | solution.py:633
  149.6 3.5 %hand_over.1 = (bf16[64,8192]{1,0:T(8,128)(2,1)}, bf16[64,1024]{1,0:T(8,128)(2,1)}, bf16[64,1024]{1,0:T(8,128)(2,1)}) custom-call(bf16[64,8192]{1,0:T(8,128)(2,1)} %get-tuple-element.6.gq_ref, bf16[64,1024]{1,0:T(8,128)(2,1)} %get-tuple-element.7.gk_ref, bf16[64,1024]{1,0:T(8,128)(2,1)} %get-tuple-element.8.gv_ref), custom_call_target="tpu_custom_call" | custom-call | tf_op jit(solution)/shard_map/hand_over/pallas_call | solution.py:671
  (6 shorter events, 0.1 us)
Async XLA Ops:
  0.6 0.7 copy-start
  0.7 0.7 copy-start.1
